TPU v7x, 32 devices: a whole 2x2x4 slice. The times are simulated.
32 devices in a mesh: dp: 8 (over y, x, core), expert: 4 (over z).
Axes of the slice: x: 2, y: 2, z: 4, core: 2. Of those that a mesh axis runs over, the one named last changes fastest.
Arguments:
- frames: bfloat16 [16384, 1024], P(('dp', 'expert')), may hold values from -6 to 6
- lengths: int32 [64], P(('dp', 'expert')), may hold values from 64 to 256, as said below
- expert_ids: int32 [16384, 1], P(('dp', 'expert')), may hold values from 0 to 3; in each aligned block of 512 rows (0 to 511, 512 to 1023, ...) at most 144 rows name the same one
- conv_kernel: float32 [31, 1024], replicated, may hold values from -1 to 1
- conv_gain: float32 [1024], replicated, may hold values from 0.25 to 1.75
- ffn_gain: float32 [1024], replicated, may hold values from 0.25 to 1.75
- w_in: bfloat16 [4, 1024, 4096], P('expert'), may hold values from -0.1875 to 0.1875
- w_out: bfloat16 [4, 4096, 1024], P('expert'), may hold values from -0.09375 to 0.09375
- out_grad: bfloat16 [16384, 1024], P(('dp', 'expert')), may hold values from -6 to 6
Outputs:
- block_out: bfloat16 [16384, 1024], P(('dp', 'expert'))
- frames_grad: bfloat16 [16384, 1024], P(('dp', 'expert'))
- w_in_grad: float32 [4, 1024, 4096], P('expert', None, 'dp')
- w_out_grad: float32 [4, 4096, 1024], P('expert', 'dp')
- kernel_grad: float32 [31, 1024], replicated
- gain_grads: float32 [2, 1024], replicated
Inputs may be any that keep to these rules, and one draw needn't show every extreme that they name: `expert_ids`: in the rows of one device (aligned blocks of 512 rows) no expert is named more than 144 times, a bound that some block reaches. `lengths`: all utterances of some device have 256 live frames.
All inputs are finite; a program needn't handle non-finite values.
Results may differ from a plain program's by a relative error of at most 0.0053.
Values may be sent and summed in bfloat16 or wider, within the bound.
A program may use at most 256 MiB of HBM per device.

v0:
```python
import jax
import jax.numpy as jnp
from jax import lax
from jax.sharding import PartitionSpec as P


def layer_norm(values, gain_vec):
    row_mean = jnp.mean(values, axis=-1, keepdims=True)
    centered = values - row_mean
    row_var = jnp.mean(centered * centered, axis=-1, keepdims=True)
    return centered * lax.rsqrt(row_var + 1e-05) * gain_vec


def conv_module(frames_f, live_mask, conv_kernel, conv_gain, ffn_gain):
    normed_conv = layer_norm(frames_f, conv_gain) * live_mask
    tap_count = conv_kernel.shape[0]
    half_span = (tap_count - 1) // 2
    utt_len = frames_f.shape[1]
    padded = jnp.pad(normed_conv, ((0, 0), (half_span, half_span), (0, 0)))
    conv_out = jnp.zeros_like(normed_conv)
    for tap_index in range(tap_count):
        conv_out = conv_out + conv_kernel[tap_index] * padded[:, tap_index : tap_index + utt_len]
    residual = frames_f + live_mask * jax.nn.silu(conv_out)
    return (residual, layer_norm(residual, ffn_gain))


def silu_slope(values):
    sig_val = jax.nn.sigmoid(values)
    return sig_val * (1.0 + values * (1.0 - sig_val))


def contract_rows(left_rows, right_rows):
    return lax.dot_general(
        left_rows, right_rows, (((0,), (0,)), ((), ())), preferred_element_type=jnp.float32
    )


def times_transpose(left_rows, matrix):
    return lax.dot_general(
        left_rows, matrix, (((1,), (1,)), ((), ())), preferred_element_type=jnp.float32
    )


def shards(frames, lengths, expert_ids, conv_kernel, conv_gain, ffn_gain, w_in, w_out, out_grad):
    utt_count = lengths.shape[0]
    frame_count = frames.shape[0]
    utt_len = frame_count // utt_count
    feat_width = frames.shape[1]
    expert_count = lax.axis_size("expert")
    capacity = max(8, 8 * (9 * frame_count // (64 * expert_count)))
    slot_total = expert_count * capacity
    live_mask = (jnp.arange(utt_len, dtype=jnp.int32)[None, :] < lengths[:, None]).astype(
        jnp.float32
    )[:, :, None]
    frames_f = frames.astype(jnp.float32).reshape(utt_count, utt_len, feat_width)
    residual, normed = conv_module(frames_f, live_mask, conv_kernel, conv_gain, ffn_gain)
    expert_in = normed.reshape(frame_count, feat_width).astype(jnp.bfloat16)
    live_flat = live_mask.reshape(frame_count) > 0.5
    target = jnp.where(live_flat, expert_ids[:, 0], expert_count)
    one_hot = (target[:, None] == jnp.arange(expert_count, dtype=jnp.int32)[None, :]).astype(
        jnp.int32
    )
    rank_in = jnp.sum((jnp.cumsum(one_hot, axis=0, dtype=jnp.int32) - 1) * one_hot, axis=1)
    dest_slot = jnp.where(live_flat, target * capacity + rank_in, slot_total)
    routed_grad = jnp.where(live_flat[:, None], out_grad, jnp.zeros_like(out_grad))
    send_in = (
        jnp.zeros((slot_total, feat_width), jnp.bfloat16).at[dest_slot].set(expert_in, mode="drop")
    )
    send_grad = (
        jnp.zeros((slot_total, feat_width), jnp.bfloat16)
        .at[dest_slot]
        .set(routed_grad, mode="drop")
    )
    recv_in, recv_grad = (
        lax.all_to_all(
            send_in.reshape(expert_count, capacity, feat_width),
            "expert",
            split_axis=0,
            concat_axis=0,
            tiled=True,
        ),
        lax.all_to_all(
            send_grad.reshape(expert_count, capacity, feat_width),
            "expert",
            split_axis=0,
            concat_axis=0,
            tiled=True,
        ),
    )
    routed_in = recv_in.reshape(slot_total, feat_width)
    grad_rows = recv_grad.reshape(slot_total, feat_width)
    weights_in = w_in[0]
    weights_out = w_out[0]
    pre_act = jnp.dot(routed_in, weights_in, preferred_element_type=jnp.float32)
    hidden = jax.nn.silu(pre_act).astype(jnp.bfloat16)
    out_rows = jnp.dot(hidden, weights_out, preferred_element_type=jnp.float32).astype(jnp.bfloat16)
    hidden_grad = times_transpose(grad_rows, weights_out)
    pre_grad = (hidden_grad * silu_slope(pre_act)).astype(jnp.bfloat16)
    back_rows = times_transpose(pre_grad, weights_in).astype(jnp.bfloat16)
    ret_out, ret_back = (
        lax.all_to_all(
            out_rows.reshape(expert_count, capacity, feat_width),
            "expert",
            split_axis=0,
            concat_axis=0,
            tiled=True,
        ),
        lax.all_to_all(
            back_rows.reshape(expert_count, capacity, feat_width),
            "expert",
            split_axis=0,
            concat_axis=0,
            tiled=True,
        ),
    )
    full_in = contract_rows(routed_in, pre_grad)
    full_out = contract_rows(hidden, grad_rows)
    grad_in, grad_out = (
        lax.psum_scatter(full_in, "dp", scatter_dimension=1, tiled=True),
        lax.psum_scatter(full_out, "dp", scatter_dimension=0, tiled=True),
    )
    safe_slot = jnp.minimum(dest_slot, slot_total - 1)
    zero_rows = jnp.zeros((frame_count, feat_width), jnp.float32)
    expert_out = jnp.where(
        live_flat[:, None],
        ret_out.reshape(slot_total, feat_width)[safe_slot].astype(jnp.float32),
        zero_rows,
    )
    expert_back = jnp.where(
        live_flat[:, None],
        ret_back.reshape(slot_total, feat_width)[safe_slot].astype(jnp.float32),
        zero_rows,
    )
    block_out = (residual.reshape(frame_count, feat_width) + expert_out).astype(jnp.bfloat16)

    def local_map(frames_in, kernel_in, gain_conv, gain_ffn):
        return conv_module(frames_in, live_mask, kernel_in, gain_conv, gain_ffn)

    unused_out, pull_back = jax.vjp(local_map, frames_f, conv_kernel, conv_gain, ffn_gain)
    frames_part, kernel_part, conv_part, ffn_part = pull_back(
        (
            out_grad.astype(jnp.float32).reshape(utt_count, utt_len, feat_width),
            expert_back.reshape(utt_count, utt_len, feat_width),
        )
    )
    kernel_grad, gain_grads = lax.psum(
        (kernel_part, jnp.stack([conv_part, ffn_part])), ("dp", "expert")
    )
    frames_grad = frames_part.reshape(frame_count, feat_width).astype(jnp.bfloat16)
    return (block_out, frames_grad, grad_in[None], grad_out[None], kernel_grad, gain_grads)


def solution(mesh):
    return jax.shard_map(
        shards,
        mesh=mesh,
        in_specs=(
            P(("dp", "expert"), None),
            P(("dp", "expert")),
            P(("dp", "expert"), None),
            P(),
            P(),
            P(),
            P("expert", None, None),
            P("expert", None, None),
            P(("dp", "expert"), None),
        ),
        out_specs=(
            P(("dp", "expert"), None),
            P(("dp", "expert"), None),
            P("expert", None, "dp"),
            P("expert", "dp", None),
            P(),
            P(),
        ),
        check_vma=False,
    )
```

profile of v0, /device:TPU:0, one launch (start us, length us, event | category | flops | bytes accessed | tf_op | source)
XLA Modules:
  0.0 445.2 jit_solution(7682977713145154705)
XLA Ops:
  8.1 1.5 convert_reduce_fusion
  9.6 1.6 multiply_reduce_fusion.34
  11.4 0.6 copy-done.19
  12.1 1.2 reduce-window.6
  13.3 0.2 slice_reduce_fusion
  13.5 0.2 reduce-window.9
  13.9 0.4 multiply_multiply_fusion
  14.3 9.5 %multiply_add_fusion = (f32[2,256,1024]{2,1,0:T(8,128)S(1)}, f32[2,256,1024]{2,1,0:T(8,128)}) fusion(f32[2,256]{1,0:T(2,128)S(1)} %get-tuple-element.113, bf16[512,1024]{1,0:T(8,128)(2,1)S(1)} %copy-done, f32[1024]{0:T(1024)S(1)} %bitcast.207, f32[1024]{0:T(1024)S(1)} %bitcast.161, f32[1024]{0:T(1024)S(1)} %bitcast.163, f32[1024]{0:T(1024)S(1)} %bitcast.165, ...), kind=kLoop, calls=%fused_computation.105 | loop fusion | flops 35651584 | bytes 7469056 | tf_op jit(solution)/shard_map/add | solution.py:23
  23.9 0.2 reduce_sum.378
  24.1 0.4 multiply_reduce_fusion.33
  24.4 0.1 copy-done.18
  24.6 1.3 multiply_convert_fusion.2
  25.9 4.4 scatter_custom_fusion
  30.2 6.3 %all-to-all-start = ((bf16[4,144,1024]{2,1,0:T(8,128)(2,1)}), bf16[4,144,1024]{2,1,0:T(8,128)(2,1)}, u32[]{:S(2)}, u32[]{:S(2)}) async-start(bf16[4,144,1024]{2,1,0:T(8,128)(2,1)} %bitcast.154), calls=%async_computation | async-start | bytes 2359296 | tf_op jit(solution)/shard_map/all_to_all | solution.py:75
  36.6 3.7 scatter_custom_fusion.1
  40.3 24.9 %all-to-all-done = bf16[4,144,1024]{2,1,0:T(8,128)(2,1)} async-done(((bf16[4,144,1024]{2,1,0:T(8,128)(2,1)}), bf16[4,144,1024]{2,1,0:T(8,128)(2,1)}, u32[]{:S(2)}, u32[]{:S(2)}) %all-to-all-start) | async-done | bytes 1179680 | tf_op jit(solution)/shard_map/all_to_all | solution.py:75
  65.2 3.7 all-to-all-start.2
  68.9 9.9 %fusion.6 = f32[576,4096]{1,0:T(8,128)} fusion(bf16[576,1024]{1,0:T(8,128)(2,1)} %bitcast.40, bf16[1,1024,4096]{2,1,0:T(8,128)(2,1)} %param.15), kind=kOutput, calls=%fused_computation.13 | convolution fusion | flops 4831838208 | bytes 19005440 | tf_op jit(solution)/shard_map/dot_general | solution.py:94
  78.8 18.1 %all-to-all-done.2 = bf16[4,144,1024]{2,1,0:T(8,128)(2,1)S(1)} async-done(((bf16[4,144,1024]{2,1,0:T(8,128)(2,1)}), bf16[4,144,1024]{2,1,0:T(8,128)(2,1)S(1)}, u32[]{:S(2)}, u32[]{:S(2)}) %all-to-all-start.2) | async-done | bytes 1179680 | tf_op jit(solution)/shard_map/all_to_all | solution.py:82
  96.9 11.2 %multiply_convert_fusion = bf16[576,4096]{1,0:T(8,128)(2,1)S(1)} fusion(f32[576,4096]{1,0:T(8,128)} %fusion.6, bf16[576,1024]{1,0:T(8,128)(2,1)S(1)} %bitcast.155, bf16[1,4096,1024]{2,1,0:T(8,128)(2,1)} %param.16), kind=kOutput, calls=%fused_computation.4 | convolution fusion | flops 4853071872 | bytes 23724032 | tf_op jit(solution)/shard_map/dot_general | solution.py:39
  108.2 10.4 %fusion.21 = bf16[576,1024]{1,0:T(8,128)(2,1)} fusion(bf16[576,4096]{1,0:T(8,128)(2,1)S(1)} %multiply_convert_fusion, bf16[1,1024,4096]{2,1,0:T(8,128)(2,1)} %param.15), kind=kOutput, calls=%fused_computation.110 | convolution fusion | flops 4832428032 | bytes 14286848 | tf_op jit(solution)/shard_map/dot_general | solution.py:39
  118.6 3.5 all-to-all-start.3
  122.1 0.3 all-reduce.65.cloned.1.call-start
  122.4 27.7 %all-to-all-done.3 = bf16[4,144,1024]{2,1,0:T(8,128)(2,1)S(1)} async-done(((bf16[4,144,1024]{2,1,0:T(8,128)(2,1)}), bf16[4,144,1024]{2,1,0:T(8,128)(2,1)S(1)}, u32[]{:S(2)}, u32[]{:S(2)}) %all-to-all-start.3) | async-done | bytes 1179680 | tf_op jit(solution)/shard_map/all_to_all | solution.py:108
  150.1 2.8 gather_fusion.1
  152.9 2.6 fusion.16
  155.6 2.0 add_add_fusion.1
  157.6 1.9 reduce_sum.384
  159.5 20.3 %multiply_reduce_fusion.30 = (f32[1024]{0:T(1024)S(1)}, f32[1024]{0:T(1024)S(1)}, f32[1024]{0:T(1024)S(1)}, f32[1024]{0:T(1024)S(1)}, f32[1024]{0:T(1024)S(1)}, ...) fusion(f32[2,256,1024]{2,1,0:T(8,128)} %copy-done.5, ...), kind=kLoop, calls=%fused_computation.99 | loop fusion | flops 27249664 | bytes 11610624 | tf_op jit(solution)/shard_map/transpose(jvp())/reduce_sum | solution.py:22
  179.8 4.9 %multiply_reduce_fusion.31 = (f32[1024]{0:T(1024)S(1)}, f32[1024]{0:T(1024)S(1)}, f32[1024]{0:T(1024)S(1)}, f32[1024]{0:T(1024)S(1)}, f32[1024]{0:T(1024)S(1)}, ...) fusion(f32[2,256,1024]{2,1,0:T(8,128)S(1)} %get-tuple-element.4, ...), kind=kLoop, calls=%fused_computation.100 | loop fusion | flops 18855936 | bytes 4268032 | tf_op jit(solution)/shard_map/transpose(jvp())/reduce_sum | solution.py:22
  184.7 0.9 pad_add_fusion.7
  185.7 0.5 reduce-scatter.5.cloned.1.call-start
  186.2 14.5 %fusion.40 = f32[4096,1024]{1,0:T(8,128)} fusion(bf16[576,1024]{1,0:T(8,128)(2,1)S(1)} %bitcast.156, f32[576,4096]{1,0:T(8,128)} %fusion.6), kind=kOutput, calls=%fused_computation.179 | convolution fusion | flops 4843634688 | bytes 27394048 | tf_op jit(solution)/shard_map/dot_general | solution.py:33
  200.7 14.4 %fusion.45 = f32[1024,4096]{1,0:T(8,128)} fusion(bf16[576,1024]{1,0:T(8,128)(2,1)} %bitcast.40, bf16[576,4096]{1,0:T(8,128)(2,1)} %copy-done.13), kind=kOutput, calls=%fused_computation.182 | convolution fusion | flops 4831838208 | bytes 22675456 | tf_op jit(solution)/shard_map/dot_general | solution.py:33
  215.1 12.6 %fusion.24 = bf16[576,1024]{1,0:T(8,128)(2,1)S(1)} fusion(bf16[1,4096,1024]{2,1,0:T(8,128)(2,1)} %param.16, f32[576,4096]{1,0:T(8,128)} %fusion.6), kind=kOutput, calls=%fused_computation.111 | convolution fusion | flops 4844224512 | bytes 19005440 | tf_op jit(solution)/shard_map/dot_general | solution.py:96
  227.7 30.6 %all_to_all.20 = bf16[4,144,1024]{2,1,0:T(8,128)(2,1)S(1)} all-to-all(bf16[4,144,1024]{2,1,0:T(8,128)(2,1)S(1)} %bitcast.158), channel_id=1, replica_groups=mesh['dp'=8,'expert'=4] {'expert'}, dimensions={0} | all-to-all | bytes 2359296 | tf_op jit(solution)/shard_map/all_to_all | solution.py:101
  258.4 2.8 gather_fusion
  261.1 10.8 %broadcast_multiply_fusion.1 = (f32[2,256,1024]{2,1,0:T(8,128)}, f32[2,256,1024]{2,1,0:T(8,128)}, f32[2,256,1024]{2,1,0:T(8,128)}, f32[2,256,1024]{2,1,0:T(8,128...) fusion(f32[2,256,1024]{2,1,0:T(8,128)} %copy-done.7, ...), kind=kLoop, calls=%fused_computation.115 | loop fusion | flops 6815744 | bytes 29413376 | tf_op jit(solution)/shard_map/transpose(jvp())/mul | solution.py:22
  271.9 12.5 %broadcast_multiply_fusion = (f32[2,256,1024]{2,1,0:T(8,128)}, f32[2,256,1024]{2,1,0:T(8,128)}, f32[2,256,1024]{2,1,0:T(8,128)}, f32[2,256,1024]{2,1,0:T(8,128)}...) fusion(f32[2,256,1024]{2,1,0:T(8,128)S(1)} %copy-done.8, ...), kind=kLoop, calls=%fused_computation.114 | loop fusion | flops 9437184 | bytes 39919616 | tf_op jit(solution)/shard_map/transpose(jvp())/mul | solution.py:22
  284.4 22.3 %pad_add_fusion = f32[2,286,1024]{2,1,0:T(8,128)} fusion(f32[2,256,1024]{2,1,0:T(8,128)} %get-tuple-element.56, f32[2,256,1024]{2,1,0:T(8,128)} %get-tuple-element.57, f32[2,256,1024]{2,1,0:T(8,128)} %get-tuple-element.58, f32[2,256,1024]{2,1,0:T(8,128)} %get-tuple-element.59, f32[2,256,1024]{2,1,0:T(8,128)} %get-tuple-element.60, ...), kind=kLoop, calls=%fused_computation.18 | loop fusion | flops 14057472 | bytes 54771712 | tf_op jit(solution)/shard_map/transpose(jvp())/add_any | solution.py:22
  306.7 6.4 %multiply_reduce_fusion.32 = (f32[2,256]{1,0:T(2,128)S(1)}, f32[2,256,1024]{2,1,0:T(8,128)S(1)}, f32[2,256,1024]{2,1,0:T(8,128)S(1)}) fusion(f32[1024]{0:T(1024)S(1)} %copy-done.17, f32[2,256]{1,0:T(2,128)S(1)} %div.54, bf16[2,256,1024]{2,1,0:T(8,128)(2,1)S(1)} %bitcast.151, f32[2,256]{1,0:T(2,128)S(1)} %get-tuple-element.113, ...), kind=kLoop, calls=%fused_computation.102 | loop fusion | flops 6290944 | bytes 19933184 | tf_op jit(solution)/shard_map/transpose(jvp())/reduce_sum | solution.py:11
  313.2 1.1 multiply_reduce_fusion
  314.3 0.2 copy-done.9
  314.5 39.0 %psum.15 = f32[2,1024]{1,0:T(2,128)} all-reduce(f32[2,1024]{1,0:T(2,128)S(1)} %pad_maximum_fusion), channel_id=1, replica_groups=mesh['dp'=8,'expert'=4] {'dp','expert'}, use_global_device_ids=true, to_apply=%region_49.50 | all-reduce | flops 2048 | bytes 16384 | tf_op jit(solution)/shard_map/psum | solution.py:146
  353.5 2.9 fusion.18
  356.4 2.4 add_convert_fusion
  358.9 77.1 %reduce-scatter.3.cloned.1.call-done = f32[1024,512]{1,0:T(8,128)} async-done(((f32[1024,4096]{1,0:T(8,128)}), f32[1024,512]{1,0:T(8,128)}) %reduce-scatter.3.cloned.1.call-update) | async-done | bytes 2097168 | tf_op jit(solution)/shard_map/reduce_scatter | solution.py:119
  436.0 1.6 copy.19
  (77 shorter events, 0.7 us)
Async XLA Ops:
  8.0 5.8 %copy-start = (bf16[512,1024]{1,0:T(8,128)(2,1)S(1)}, bf16[512,1024]{1,0:T(8,128)(2,1)}, u32[]{:S(2)}) copy-start(bf16[512,1024]{1,0:T(8,128)(2,1)} %param.9) | copy-start | bytes 3145732
  8.0 3.2 copy-start.16
  8.0 3.9 copy-start.24
  8.0 4.0 copy-start.21
  8.0 5.8 %copy-start.17 = (f32[1024]{0:T(1024)S(1)}, f32[1024]{0:T(1024)}, u32[]{:S(2)}) copy-start(f32[1024]{0:T(1024)} %param.13) | copy-start | bytes 12292
  11.4 0.6 copy-start.19
  14.3 9.6 %copy-start.5 = (f32[2,256,1024]{2,1,0:T(8,128)}, f32[2,256,1024]{2,1,0:T(8,128)S(1)}, u32[]{:S(2)}) copy-start(f32[2,256,1024]{2,1,0:T(8,128)S(1)} %multiply_multiply_fusion) | copy-start | bytes 6291460
  23.9 0.7 copy-start.18
  25.9 10.7 %copy-start.11 = (bf16[512,1024]{1,0:T(8,128)(2,1)S(1)}, bf16[512,1024]{1,0:T(8,128)(2,1)}, u32[]{:S(2)}) copy-start(bf16[512,1024]{1,0:T(8,128)(2,1)} %param.17) | copy-start | bytes 3145732
  30.2 35.0 %all-to-all-start = ((bf16[4,144,1024]{2,1,0:T(8,128)(2,1)}), bf16[4,144,1024]{2,1,0:T(8,128)(2,1)}, u32[]{:S(2)}, u32[]{:S(2)}) async-start(bf16[4,144,1024]{2,1,0:T(8,128)(2,1)} %bitcast.154), calls=%async_computation | async-start | bytes 2359296 | tf_op jit(solution)/shard_map/all_to_all | solution.py:75
  36.6 28.6 %copy-start.22 = (pred[512]{0:T(512)(128)(4,1)}, pred[512]{0:T(512)(128)(4,1)S(1)}, u32[]{:S(2)}) copy-start(pred[512]{0:T(512)(128)(4,1)S(1)} %gt.26) | copy-start | bytes 1540
  65.2 31.7 %all-to-all-start.2 = ((bf16[4,144,1024]{2,1,0:T(8,128)(2,1)}), bf16[4,144,1024]{2,1,0:T(8,128)(2,1)S(1)}, u32[]{:S(2)}, u32[]{:S(2)}) async-start(bf16[4,144,1024]{2,1,0:T(8,128)(2,1)} %bitcast.153), calls=%async_computation.2 | async-start | bytes 2359296 | tf_op jit(solution)/shard_map/all_to_all | solution.py:82
  96.9 11.2 %copy-start.14 = (bf16[4,144,1024]{2,1,0:T(8,128)(2,1)}, bf16[4,144,1024]{2,1,0:T(8,128)(2,1)S(1)}, u32[]{:S(2)}) copy-start(bf16[4,144,1024]{2,1,0:T(8,128)(2,1)S(1)} %all-to-all-done.2) | copy-start | bytes 3538948
  108.2 10.4 %copy-start.13 = (bf16[576,4096]{1,0:T(8,128)(2,1)}, bf16[576,4096]{1,0:T(8,128)(2,1)S(1)}, u32[]{:S(2)}) copy-start(bf16[576,4096]{1,0:T(8,128)(2,1)S(1)} %multiply_convert_fusion) | copy-start | bytes 14155780
  118.6 31.5 %all-to-all-start.3 = ((bf16[4,144,1024]{2,1,0:T(8,128)(2,1)}), bf16[4,144,1024]{2,1,0:T(8,128)(2,1)S(1)}, u32[]{:S(2)}, u32[]{:S(2)}) async-start(bf16[4,144,1024]{2,1,0:T(8,128)(2,1)} %bitcast.157), calls=%async_computation.3 | async-start | bytes 2359296 | tf_op jit(solution)/shard_map/all_to_all | solution.py:108
  122.1 236.8 %all-reduce.65.cloned.1.call-start = ((), (), s32[]{:S(2)}) async-start(), calls=%async_computation.8 | async-start | bytes 262144 | tf_op jit(solution)/shard_map/psum | solution.py:146
  152.9 2.7 copy-start.3
  157.6 1.9 copy-start.1
  159.4 20.4 %copy-start.6 = (f32[2,256,1024]{2,1,0:T(8,128)S(1)}, f32[2,256,1024]{2,1,0:T(8,128)}, u32[]{:S(2)}) copy-start(f32[2,256,1024]{2,1,0:T(8,128)} %copy-done.5) | copy-start | bytes 6291460
  179.8 4.9 %copy-start.7 = (f32[2,256,1024]{2,1,0:T(8,128)}, f32[2,256,1024]{2,1,0:T(8,128)S(1)}, u32[]{:S(2)}) copy-start(f32[2,256,1024]{2,1,0:T(8,128)S(1)} %get-tuple-element.41) | copy-start | bytes 6291460
  179.8 6.4 %copy-start.15 = (bf16[4,144,1024]{2,1,0:T(8,128)(2,1)S(1)}, bf16[4,144,1024]{2,1,0:T(8,128)(2,1)}, u32[]{:S(2)}) copy-start(bf16[4,144,1024]{2,1,0:T(8,128)(2,1)} %copy-done.14) | copy-start | bytes 3538948
  185.7 173.2 %reduce-scatter.5.cloned.1.call-start = ((), (), s32[]{:S(2)}) async-start(), calls=%async_computation.7 | async-start | bytes 18874368 | tf_op jit(solution)/shard_map/reduce_scatter | solution.py:120
  200.7 235.3 %reduce-scatter.3.cloned.1.call-start = ((), (), s32[]{:S(2)}) async-start(), calls=%async_computation.6 | async-start | bytes 18874368 | tf_op jit(solution)/shard_map/reduce_scatter | solution.py:119
  261.1 10.8 %copy-start.8 = (f32[2,256,1024]{2,1,0:T(8,128)S(1)}, f32[2,256,1024]{2,1,0:T(8,128)}, u32[]{:S(2)}) copy-start(f32[2,256,1024]{2,1,0:T(8,128)} %copy-done.7) | copy-start | bytes 6291460
  284.3 22.4 %copy-start.2 = (bf16[512,1024]{1,0:T(8,128)(2,1)S(1)}, bf16[512,1024]{1,0:T(8,128)(2,1)}, u32[]{:S(2)}) copy-start(bf16[512,1024]{1,0:T(8,128)(2,1)} %param.9) | copy-start | bytes 3145732
  306.7 6.4 %copy-start.20 = (f32[2,256]{1,0:T(2,128)S(1)}, f32[2,256]{1,0:T(2,128)}, u32[]{:S(2)}) copy-start(f32[2,256]{1,0:T(2,128)} %copy-done.19) | copy-start | bytes 6148
  313.1 1.3 copy-start.9
  313.2 40.3 %copy-start.23 = (pred[512]{0:T(512)(128)(4,1)S(1)}, pred[512]{0:T(512)(128)(4,1)}, u32[]{:S(2)}) copy-start(pred[512]{0:T(512)(128)(4,1)} %copy-done.22) | copy-start | bytes 1540
  353.5 2.9 copy-start.4
  353.5 2.9 copy-start.10
  353.5 2.9 copy-start.12
Sparse Core Ops, SparseCore 0:
  185.8 142.2 all-reduce.64
Sparse Core Ops, SparseCore 1:
  200.8 115.3 reduce-scatter.4
  320.1 115.8 reduce-scatter.2
where the time goes:
time: 453 us; the launch traced here: 445 us
  waiting for transfers between devices  148 us (33%)
  other arithmetic  111 us (25%)
  matrix products  72.9 us (16%)
  blocking collectives  69.6 us (15%)
  between operations  16.1 us (4%)
  starting transfers between devices  14.4 us (3%)
  local copies, waits for them, and re-layouts  12.9 us (3%)
    reduce_scatter x1, waiting for transfers between devices, shards(): lax.psum_scatter(full_in, 'dp', scatter_dimension=1, tiled=True)  77.1 us
    psum x1, blocking collectives, shards(): lax.psum((kernel_part, jnp.stack([conv_part, ffn_part])), ('dp', 'expert'))  39 us
    all_to_all x1, blocking collectives, shards(): lax.all_to_all(out_rows.reshape(expert_count, capacity, feat_width), 'exp...  30.6 us
    dot_general x2, matrix products, contract_rows(): lax.dot_general(left_rows, right_rows, (((0,), (0,)), ((), ())), preferre...  28.9 us
    all_to_all x1, waiting for transfers between devices, shards(): lax.all_to_all(back_rows.reshape(expert_count, capacity, feat_width), 'ex...  27.7 us
    reduce_sum x2, other arithmetic, conv_module(): conv_kernel[tap_index] * padded[:, tap_index:tap_index + utt_len]  25.2 us
    all_to_all x1, waiting for transfers between devices, shards(): lax.all_to_all(send_in.reshape(expert_count, capacity, feat_width), 'expe...  24.9 us
    mul x2, other arithmetic, conv_module(): conv_kernel[tap_index] * padded[:, tap_index:tap_index + utt_len]  23.2 us
  transfers between devices with their start and end apart: 6, of which 4 were waited for; matrix products, arithmetic and copies ran while one was open for 26% of the time, Pallas kernels for 0%

commit v1 on v0

v1 whole, which is shorter than its diff:
```python
import jax
import jax.numpy as jnp
from jax import lax
from jax.experimental import pallas as pl
from jax.experimental.pallas import tpu as pltpu
from jax.sharding import PartitionSpec as P

LANES = 128
EDGE = 16
ROWS = 32
F32 = jnp.float32
BF16 = jnp.bfloat16


def lane_slice(index):
    return pl.ds(pl.multiple_of(index * LANES, LANES), LANES)


def row_slice(start, count):
    return pl.ds(pl.multiple_of(start, ROWS), count)


def centred(values):
    row_mean = jnp.mean(values, axis=-1, keepdims=True)
    shifted = values - row_mean
    row_var = jnp.mean(shifted * shifted, axis=-1, keepdims=True)
    return shifted, lax.rsqrt(row_var + 1e-05)


def live_rows(start, count, length):
    return ((start + lax.broadcasted_iota(jnp.int32, (count, 1), 0)) < length).astype(F32)


def clear_edges(padded_ref, utt_len):
    zeros = jnp.zeros((padded_ref.shape[0], EDGE, LANES), F32)
    padded_ref[:, 0:EDGE, :] = zeros
    padded_ref[:, EDGE + utt_len :, :] = zeros


def scatter_lanes(padded_ref, start, count, values):
    for chunk in range(padded_ref.shape[0]):
        padded_ref[chunk, pl.ds(pl.multiple_of(start + EDGE, EDGE), count), :] = values[
            :, chunk * LANES : (chunk + 1) * LANES
        ]


def conv_forward_kernel(len_ref, x_ref, taps_ref, gain_ref, ffn_ref, res_ref, conv_ref, in_ref, pad_ref):
    length = len_ref[pl.program_id(0)]
    utt_len, width = x_ref.shape
    tap_count = taps_ref.shape[0]
    shift = EDGE - (tap_count - 1) // 2
    chunks = width // LANES
    clear_edges(pad_ref, utt_len)

    @pl.loop(0, utt_len // ROWS)
    def _(step):
        start = step * ROWS
        shifted, scale = centred(x_ref[row_slice(start, ROWS), :].astype(F32))
        normed = shifted * scale * gain_ref[...] * live_rows(start, ROWS, length)
        scatter_lanes(pad_ref, start, ROWS, normed)

    block = 64

    @pl.loop(0, chunks)
    def _(chunk):
        lanes = lane_slice(chunk)

        @pl.loop(0, utt_len // block)
        def _(step):
            start = step * block
            total = jnp.zeros((block, LANES), F32)
            for tap in range(tap_count):
                total = total + taps_ref[tap : tap + 1, lanes] * pad_ref[chunk, pl.ds(start + tap + shift, block), :]
            rows = row_slice(start, block)
            conv_ref[rows, lanes] = total
            silu = total * (1.0 / (1.0 + jnp.exp(-total)))
            res_ref[rows, lanes] = x_ref[rows, lanes].astype(F32) + live_rows(start, block, length) * silu

    @pl.loop(0, utt_len // ROWS)
    def _(step):
        rows = row_slice(step * ROWS, ROWS)
        shifted, scale = centred(res_ref[rows, :])
        in_ref[rows, :] = (shifted * scale * ffn_ref[...]).astype(BF16)


def fold_rows(values):
    return jnp.sum(values.reshape(values.shape[0] // 8, 8, values.shape[1]), axis=0)


def conv_backward_kernel(
    len_ref, x_ref, taps_ref, gain_ref, ffn_ref, res_ref, conv_ref, back_ref, grad_ref,
    out_ref, sums_ref, pad_ref, dpad_ref, dres_ref, dnorm_ref, gains_ref,
):
    utt = pl.program_id(0)
    length = len_ref[utt]
    utt_len, width = x_ref.shape
    tap_count = taps_ref.shape[0]
    half = (tap_count - 1) // 2
    chunks = width // LANES
    clear_edges(pad_ref, utt_len)
    clear_edges(dpad_ref, utt_len)

    @pl.when(utt == 0)
    def _():
        sums_ref[...] = jnp.zeros_like(sums_ref)
        gains_ref[...] = jnp.zeros_like(gains_ref)

    @pl.loop(0, utt_len // ROWS)
    def _(step):
        start = step * ROWS
        rows = row_slice(start, ROWS)
        live = live_rows(start, ROWS, length)
        shifted, scale = centred(x_ref[rows, :].astype(F32))
        scatter_lanes(pad_ref, start, ROWS, shifted * scale * gain_ref[...] * live)

    @pl.loop(0, utt_len // ROWS)
    def _(step):
        start = step * ROWS
        rows = row_slice(start, ROWS)
        live = live_rows(start, ROWS, length)
        shifted, scale = centred(res_ref[rows, :])
        unit = shifted * scale
        back = back_ref[rows, :].astype(F32)
        gains_ref[1] += fold_rows(back * unit)
        scaled = back * ffn_ref[...]
        mean_scaled = jnp.mean(scaled, axis=-1, keepdims=True)
        mean_product = jnp.mean(scaled * unit, axis=-1, keepdims=True)
        dres = grad_ref[rows, :].astype(F32) + scale * (scaled - mean_scaled - unit * mean_product)
        dres_ref[rows, :] = dres
        conv = conv_ref[rows, :]
        sig = 1.0 / (1.0 + jnp.exp(-conv))
        scatter_lanes(dpad_ref, start, ROWS, dres * live * (sig * (1.0 + conv * (1.0 - sig))))

    block = 32

    @pl.loop(0, chunks)
    def _(chunk):
        lanes = lane_slice(chunk)

        @pl.loop(0, utt_len // block)
        def _(step):
            start = step * block
            total = jnp.zeros((block, LANES), F32)
            for tap in range(tap_count):
                offset = EDGE + half - tap
                total = total + taps_ref[tap : tap + 1, lanes] * dpad_ref[chunk, pl.ds(start + offset, block), :]
            dnorm_ref[row_slice(start, block), lanes] = total

        def add_taps(step, totals):
            start = step * 16
            totals = list(totals)
            for part in range(2):
                cot = dpad_ref[chunk, pl.ds(pl.multiple_of(start + EDGE + 8 * part, 8), 8), :]
                for tap in range(tap_count):
                    offset = EDGE - half + tap + 8 * part
                    totals[tap] = totals[tap] + cot * pad_ref[chunk, pl.ds(start + offset, 8), :]
            return tuple(totals)

        totals = lax.fori_loop(
            0, utt_len // 16, add_taps, tuple(jnp.zeros((8, LANES), F32) for _ in range(tap_count))
        )
        for tap in range(tap_count):
            sums_ref[tap : tap + 1, lanes] += jnp.sum(totals[tap], axis=0, keepdims=True)

    @pl.loop(0, utt_len // ROWS)
    def _(step):
        start = step * ROWS
        rows = row_slice(start, ROWS)
        live = live_rows(start, ROWS, length)
        shifted, scale = centred(x_ref[rows, :].astype(F32))
        unit = shifted * scale
        dnorm = dnorm_ref[rows, :] * live
        gains_ref[0] += fold_rows(dnorm * unit)
        scaled = dnorm * gain_ref[...]
        mean_scaled = jnp.mean(scaled, axis=-1, keepdims=True)
        mean_product = jnp.mean(scaled * unit, axis=-1, keepdims=True)
        out_ref[rows, :] = (
            dres_ref[rows, :] + scale * (scaled - mean_scaled - unit * mean_product)
        ).astype(BF16)

    @pl.when(utt == pl.num_programs(0) - 1)
    def _():
        sums_ref[tap_count : tap_count + 1, :] = jnp.sum(gains_ref[0], axis=0, keepdims=True)
        sums_ref[tap_count + 1 : tap_count + 2, :] = jnp.sum(gains_ref[1], axis=0, keepdims=True)


def conv_specs(utt_len, width, tap_count):
    rows = pl.BlockSpec((utt_len, width), lambda utt: (utt, 0))
    vector = pl.BlockSpec((1, width), lambda utt: (0, 0))
    taps = pl.BlockSpec((tap_count, width), lambda utt: (0, 0))
    return rows, vector, taps


def conv_forward(frames, lengths, taps, gain, ffn):
    frame_count, width = frames.shape
    utt_count = lengths.shape[0]
    utt_len = frame_count // utt_count
    rows, vector, tap_spec = conv_specs(utt_len, width, taps.shape[0])
    return pl.pallas_call(
        conv_forward_kernel,
        grid=(utt_count,),
        out_shape=[
            jax.ShapeDtypeStruct((frame_count, width), F32),
            jax.ShapeDtypeStruct((frame_count, width), F32),
            jax.ShapeDtypeStruct((frame_count, width), BF16),
        ],
        in_specs=[pl.BlockSpec(memory_space=pltpu.SMEM), rows, tap_spec, vector, vector],
        out_specs=[rows, rows, rows],
        scratch_shapes=[pltpu.VMEM((width // LANES, utt_len + 2 * EDGE, LANES), F32)],
        compiler_params=pltpu.CompilerParams(vmem_limit_bytes=40 << 20),
        cost_estimate=pl.CostEstimate(flops=8 << 30, bytes_accessed=40 << 20, transcendentals=0),
        name="conv_forward",
    )(lengths, frames, taps, gain, ffn)


def conv_backward(frames, lengths, taps, gain, ffn, residual, conv_out, back, out_grad):
    frame_count, width = frames.shape
    utt_count = lengths.shape[0]
    utt_len = frame_count // utt_count
    tap_count = taps.shape[0]
    rows, vector, tap_spec = conv_specs(utt_len, width, tap_count)
    padded = pltpu.VMEM((width // LANES, utt_len + 2 * EDGE, LANES), F32)
    return pl.pallas_call(
        conv_backward_kernel,
        grid=(utt_count,),
        out_shape=[
            jax.ShapeDtypeStruct((frame_count, width), BF16),
            jax.ShapeDtypeStruct((tap_count + 2, width), F32),
        ],
        in_specs=[pl.BlockSpec(memory_space=pltpu.SMEM), rows, tap_spec, vector, vector, rows, rows, rows, rows],
        out_specs=[rows, pl.BlockSpec((tap_count + 2, width), lambda utt: (0, 0))],
        scratch_shapes=[
            padded,
            padded,
            pltpu.VMEM((utt_len, width), F32),
            pltpu.VMEM((utt_len, width), F32),
            pltpu.VMEM((2, 8, width), F32),
        ],
        compiler_params=pltpu.CompilerParams(vmem_limit_bytes=40 << 20),
        cost_estimate=pl.CostEstimate(flops=8 << 30, bytes_accessed=80 << 20, transcendentals=0),
        name="conv_backward",
    )(lengths, frames, taps, gain, ffn, residual, conv_out, back, out_grad)


def silu_slope(values):
    sig_val = jax.nn.sigmoid(values)
    return sig_val * (1.0 + values * (1.0 - sig_val))


def contract_rows(left_rows, right_rows):
    return lax.dot_general(left_rows, right_rows, (((0,), (0,)), ((), ())), preferred_element_type=F32)


def times_transpose(left_rows, matrix):
    return lax.dot_general(left_rows, matrix, (((1,), (1,)), ((), ())), preferred_element_type=F32)


def exchange(rows):
    return lax.all_to_all(rows, "expert", split_axis=0, concat_axis=0, tiled=True)


def shards(frames, lengths, expert_ids, conv_kernel, conv_gain, ffn_gain, w_in, w_out, out_grad):
    utt_count = lengths.shape[0]
    frame_count, width = frames.shape
    utt_len = frame_count // utt_count
    expert_count = lax.axis_size("expert")
    capacity = max(8, 8 * (9 * frame_count // (64 * expert_count)))
    slot_total = expert_count * capacity
    taps = conv_kernel.shape[0]
    gain = conv_gain.reshape(1, width)
    ffn = ffn_gain.reshape(1, width)

    live_flat = (jnp.arange(utt_len, dtype=jnp.int32)[None, :] < lengths[:, None]).reshape(frame_count)
    target = jnp.where(live_flat, expert_ids[:, 0], expert_count)
    one_hot = (target[:, None] == jnp.arange(expert_count, dtype=jnp.int32)[None, :]).astype(jnp.int32)
    rank_in = jnp.sum((jnp.cumsum(one_hot, axis=0, dtype=jnp.int32) - 1) * one_hot, axis=1)
    dest_slot = jnp.where(live_flat, target * capacity + rank_in, slot_total)
    placing = (jnp.arange(slot_total, dtype=jnp.int32)[:, None] == dest_slot[None, :]).astype(BF16)

    send_grad = jnp.dot(placing, out_grad, preferred_element_type=F32).astype(BF16)
    grad_rows = exchange(send_grad)
    residual, conv_out, expert_in = conv_forward(frames, lengths, conv_kernel, gain, ffn)
    send_in = jnp.dot(placing, expert_in, preferred_element_type=F32).astype(BF16)
    send_in, grad_rows = lax.optimization_barrier((send_in, grad_rows))
    routed_in = exchange(send_in)
    weights_in = w_in[0]
    weights_out = w_out[0]
    hidden_grad = times_transpose(grad_rows, weights_out)
    pre_act = jnp.dot(routed_in, weights_in, preferred_element_type=F32)
    hidden = jax.nn.silu(pre_act).astype(BF16)
    pre_grad = (hidden_grad * silu_slope(pre_act)).astype(BF16)
    back_rows = times_transpose(pre_grad, weights_in).astype(BF16)
    ret_back = exchange(back_rows)
    pre_grad, back_rows = lax.optimization_barrier((pre_grad, back_rows))
    full_in = contract_rows(routed_in, pre_grad).astype(BF16)
    full_out = contract_rows(hidden, grad_rows).astype(BF16)
    grad_in = lax.psum_scatter(full_in, "dp", scatter_dimension=1, tiled=True).astype(F32)
    grad_out = lax.psum_scatter(full_out, "dp", scatter_dimension=0, tiled=True).astype(F32)
    hidden, full_in, full_out, ret_back = lax.optimization_barrier((hidden, full_in, full_out, ret_back))
    out_rows = jnp.dot(hidden, weights_out, preferred_element_type=F32).astype(BF16)
    ret_out = exchange(out_rows)

    expert_back = contract_rows(placing, ret_back).astype(BF16)
    frames_grad, sums = conv_backward(
        frames, lengths, conv_kernel, gain, ffn, residual, conv_out, expert_back, out_grad
    )
    block_out = (residual + contract_rows(placing, ret_out)).astype(BF16)
    sums = lax.psum(sums, ("dp", "expert"))
    return (block_out, frames_grad, grad_in[None], grad_out[None], sums[:taps], sums[taps:])


def solution(mesh):
    return jax.shard_map(
        shards,
        mesh=mesh,
        in_specs=(
            P(("dp", "expert"), None),
            P(("dp", "expert")),
            P(("dp", "expert"), None),
            P(),
            P(),
            P(),
            P("expert", None, None),
            P("expert", None, None),
            P(("dp", "expert"), None),
        ),
        out_specs=(
            P(("dp", "expert"), None),
            P(("dp", "expert"), None),
            P("expert", None, "dp"),
            P("expert", "dp", None),
            P(),
            P(),
        ),
        check_vma=False,
    )
```

time: 453 us -> 354 us (0.78); the launches traced: 445 us -> 352 us
  other arithmetic: 111 us -> 9.34 us
  Pallas kernels: 0 us -> 42.6 us
  blocking collectives: 69.6 us -> 31.5 us
  waiting for transfers between devices: 148 us -> 158 us
    psum x1, waiting for transfers between devices: 0.01 us -> 143 us  [shards(): sums = lax.psum(sums, ('dp', 'expert'))]
    reduce_scatter x1, waiting for transfers between devices: 77.1 us -> 0.01 us  [shards(): lax.psum_scatter(full_in, 'dp', scatter_dimension=1, tiled=True).astype(F32)]
    all_to_all x3, waiting for transfers between devices: 70.7 us -> 14.3 us  [exchange(): lax.all_to_all(rows, 'expert', split_axis=0, concat_axis=0, tiled=True)]
    pallas_call x0 -> x2, Pallas kernels: none -> 42.6 us  [the longest x1 28.2 us: conv_backward(): pl.pallas_call(conv_backward_kernel, grid=(utt_count,), out_shape=[jax.Sh...]
    reduce_sum x10 -> x0, other arithmetic: 40.9 us -> none  [the longest x2 25.2 us: conv_module(): conv_kernel[tap_index] * padded[:, tap_index:tap_index + utt_len]]
    psum x1 -> x0, blocking collectives: 39 us -> none  [shards(): lax.psum((kernel_part, jnp.stack([conv_part, ffn_part])), ('dp', 'expert'))]
    add_any x3 -> x0, other arithmetic: 25.2 us -> none  [the longest x1 22.3 us: conv_module(): padded[:, tap_index:tap_index + utt_len]]
    mul x3 -> x0, other arithmetic: 23.6 us -> none  [the longest x2 23.2 us: conv_module(): conv_kernel[tap_index] * padded[:, tap_index:tap_index + utt_len]]
  transfers between devices with their start and end apart: 6 -> 6, of which waited for: 4 -> 3; matrix products, arithmetic and copies ran while one was open for 26% -> 12% of each run, Pallas kernels for 0% -> 4%
where the time goes in v1:
time: 354 us; the launch traced here: 352 us
  waiting for transfers between devices  158 us (45%)
  matrix products  70.9 us (20%)
  Pallas kernels  42.6 us (12%)
  blocking collectives  31.5 us (9%)
  between operations  15.7 us (4%)
  starting transfers between devices  14.5 us (4%)
  other arithmetic  9.34 us (3%)
  local copies, waits for them, and re-layouts  9.1 us (3%)
    psum x1, waiting for transfers between devices, shards(): sums = lax.psum(sums, ('dp', 'expert'))  143 us
    all_to_all x1, blocking collectives, exchange(): lax.all_to_all(rows, 'expert', split_axis=0, concat_axis=0, tiled=True)  31.5 us
    pallas_call x1, Pallas kernels, conv_backward(): pl.pallas_call(conv_backward_kernel, grid=(utt_count,), out_shape=[jax.Sh...  28.2 us
    dot_general x4, matrix products, contract_rows(): lax.dot_general(left_rows, right_rows, (((0,), (0,)), ((), ())), preferre...  27 us
    dot_general x2, matrix products, times_transpose(): lax.dot_general(left_rows, matrix, (((1,), (1,)), ((), ())), preferred_el...  17.1 us
    pallas_call x1, Pallas kernels, conv_forward(): pl.pallas_call(conv_forward_kernel, grid=(utt_count,), out_shape=[jax.Sha...  14.4 us
    all_to_all x3, waiting for transfers between devices, exchange(): lax.all_to_all(rows, 'expert', split_axis=0, concat_axis=0, tiled=True)  14.3 us
    all_to_all x3, starting transfers between devices, exchange(): lax.all_to_all(rows, 'expert', split_axis=0, concat_axis=0, tiled=True)  14.2 us
  transfers between devices with their start and end apart: 6, of which 3 were waited for; matrix products, arithmetic and copies ran while one was open for 12% of the time, Pallas kernels for 4%

profile of v1, /device:TPU:0, one launch (start us, length us, event | category | flops | bytes accessed | tf_op | source)
XLA Modules:
  0.0 351.7 jit_solution(4141624002032892384)
XLA Ops:
  8.0 0.0 copy-start
  8.0 0.0 copy-start.4
  8.0 0.8 fusion.23
  8.9 0.7 broadcast_select_fusion
  9.6 1.2 reduce-window.6
  10.8 0.2 slice_reduce_fusion
  11.0 0.2 reduce-window.9
  11.2 0.1 add_bitcast_fusion
  11.3 0.7 add_select_fusion
  12.0 3.0 convolution_convert_fusion.2
  15.0 6.3 %all-to-all-start = ((bf16[4,144,1024]{2,1,0:T(8,128)(2,1)}), bf16[4,144,1024]{2,1,0:T(8,128)(2,1)S(1)}, u32[]{:S(2)}, u32[]{:S(2)}) async-start(bf16[4,144,1024]{2,1,0:T(8,128)(2,1)} %bitcast.6), calls=%async_computation | async-start | bytes 2359296 | tf_op jit(solution)/shard_map/all_to_all | solution.py:259
  21.4 0.0 copy-done.3
  21.4 0.0 copy-done.1
  21.4 14.4 %conv_forward.1 = (f32[512,1024]{1,0:T(8,128)S(1)}, f32[512,1024]{1,0:T(8,128)S(1)}, bf16[512,1024]{1,0:T(8,128)(2,1)S(1)}) custom-call(s32[2]{0:T(128)S(1)} %copy-done, bf16[512,1024]{1,0:T(8,128)(2,1)S(1)} %copy-done.1, f32[31,1024]{1,0:T(8,128)S(1)} %copy-done.3, f32[1,1024]{1,0:T(1,128)S(1)} %bitcast.69, f32[1,1024]{1,0:T(1,128)S(1)} %bitcast.71), custom_call_target="tpu_custom_call" | custom-call | flops 8589934592 | bytes 41943040 | tf_op jit(solution)/shard_map/conv_forward/pallas_call | solution.py:199
  35.8 0.0 copy-start.6
  35.8 1.3 copy-done.6
  37.1 1.3 copy-done.9
  38.4 1.8 convolution_convert_fusion.3
  40.3 9.6 %all-to-all-done = bf16[4,144,1024]{2,1,0:T(8,128)(2,1)S(1)} async-done(((bf16[4,144,1024]{2,1,0:T(8,128)(2,1)}), bf16[4,144,1024]{2,1,0:T(8,128)(2,1)S(1)}, u32[]{:S(2)}, u32[]{:S(2)}) %all-to-all-start) | async-done | bytes 1179680 | tf_op jit(solution)/shard_map/all_to_all | solution.py:259
  49.9 31.5 %all_to_all.48 = bf16[4,144,1024]{2,1,0:T(8,128)(2,1)S(1)} all-to-all(bf16[4,144,1024]{2,1,0:T(8,128)(2,1)} %bitcast.79), channel_id=1, replica_groups=mesh['dp'=8,'expert'=4] {'expert'}, dimensions={0} | all-to-all | bytes 2359296 | tf_op jit(solution)/shard_map/all_to_all | solution.py:259
  81.4 12.1 %multiply_convert_fusion.1 = (bf16[576,4096]{1,0:T(8,128)(2,1)}, f32[576,4096]{1,0:T(8,128)}) fusion(bf16[576,1024]{1,0:T(8,128)(2,1)S(1)} %bitcast.76, bf16[1,1024,4096]{2,1,0:T(8,128)(2,1)} %param.15), kind=kOutput, calls=%fused_computation.1 | convolution fusion | flops 4843634688 | bytes 23724032 | tf_op jit(solution)/shard_map/dot_general | solution.py:289
  93.6 11.0 %multiply_convert_fusion = bf16[576,4096]{1,0:T(8,128)(2,1)S(1)} fusion(f32[576,4096]{1,0:T(8,128)} %get-tuple-element.29, bf16[576,1024]{1,0:T(8,128)(2,1)S(1)} %bitcast.73, bf16[1,4096,1024]{2,1,0:T(8,128)(2,1)} %param.16), kind=kOutput, calls=%fused_computation | convolution fusion | flops 4853071872 | bytes 23724032 | tf_op jit(solution)/shard_map/dot_general | solution.py:255
  104.6 6.1 %fusion.10 = bf16[576,1024]{1,0:T(8,128)(2,1)} fusion(bf16[576,4096]{1,0:T(8,128)(2,1)S(1)} %multiply_convert_fusion, bf16[1,1024,4096]{2,1,0:T(8,128)(2,1)S(1)} %bitcast.86), kind=kOutput, calls=%fused_computation.14 | convolution fusion | flops 4832428032 | bytes 14286848 | tf_op jit(solution)/shard_map/dot_general | solution.py:255
  110.7 4.3 %all-to-all-start.2 = ((bf16[4,144,1024]{2,1,0:T(8,128)(2,1)}), bf16[4,144,1024]{2,1,0:T(8,128)(2,1)}, u32[]{:S(2)}, u32[]{:S(2)}) async-start(bf16[4,144,1024]{2,1,0:T(8,128)(2,1)} %bitcast.12), calls=%async_computation.2 | async-start | bytes 2359296 | tf_op jit(solution)/shard_map/all_to_all | solution.py:259
  115.0 0.3 all-reduce.2.cloned.1.call-start
  115.3 11.3 %convolution_convert_fusion = bf16[1024,4096]{1,0:T(8,128)(2,1)} fusion(bf16[576,1024]{1,0:T(8,128)(2,1)S(1)} %bitcast.77, bf16[576,4096]{1,0:T(8,128)(2,1)} %copy-done.11), kind=kOutput, calls=%fused_computation.11 | convolution fusion | flops 4836032512 | bytes 14286848 | tf_op jit(solution)/shard_map/dot_general | solution.py:251
  126.6 11.4 %convolution_convert_fusion.1 = bf16[4096,1024]{1,0:T(8,128)(2,1)} fusion(bf16[576,4096]{1,0:T(8,128)(2,1)} %get-tuple-element.21, bf16[576,1024]{1,0:T(8,128)(2,1)S(1)} %bitcast.74), kind=kOutput, calls=%fused_computation.12 | convolution fusion | flops 4836032512 | bytes 14286848 | tf_op jit(solution)/shard_map/dot_general | solution.py:251
  138.0 4.6 %all-to-all-done.2 = bf16[4,144,1024]{2,1,0:T(8,128)(2,1)} async-done(((bf16[4,144,1024]{2,1,0:T(8,128)(2,1)}), bf16[4,144,1024]{2,1,0:T(8,128)(2,1)}, u32[]{:S(2)}, u32[]{:S(2)}) %all-to-all-start.2) | async-done | bytes 1179680 | tf_op jit(solution)/shard_map/all_to_all | solution.py:259
  142.7 2.3 convolution_convert_fusion.4.back_ref
  145.0 0.0 copy-start.7
  145.0 1.6 copy-done.7
  146.6 1.6 copy-done.10
  148.2 28.2 %conv_backward.1 = (bf16[512,1024]{1,0:T(8,128)(2,1)}, f32[33,1024]{1,0:T(8,128)}) custom-call(s32[2]{0:T(128)S(1)} %copy-done, bf16[512,1024]{1,0:T(8,128)(2,1)S(1)} %copy-done.1, f32[31,1024]{1,0:T(8,128)S(1)} %copy-done.3, f32[1,1024]{1,0:T(1,128)S(1)} %bitcast.70, f32[1,1024]{1,0:T(1,128)S(1)} %bitcast.72, f32[512,1024]{1,0:T(8,128)S(1)} %copy-done.7, ...), custom_call_target="tpu_custom_call" | custom-call | flops 8589934592 | bytes 83886080 | tf_op jit(solution)/shard_map/conv_backward/pallas_call | solution.py:223
  176.4 0.0 all-reduce.2.cloned.1.call-update
  176.5 0.0 reduce-scatter.3.cloned.1.call-start
  176.5 0.5 reduce-scatter.3.cloned.1.call-update
  177.0 0.0 reduce-scatter.5.cloned.1.call-start
  177.1 0.5 reduce-scatter.5.cloned.1.call-update
  177.6 0.0 copy-start.8
  177.6 9.8 %fusion.13 = bf16[576,1024]{1,0:T(8,128)(2,1)} fusion(bf16[576,4096]{1,0:T(8,128)(2,1)} %get-tuple-element.21, bf16[1,4096,1024]{2,1,0:T(8,128)(2,1)} %param.16), kind=kOutput, calls=%fused_computation.15 | convolution fusion | flops 4832428032 | bytes 14286848 | tf_op jit(solution)/shard_map/dot_general | solution.py:300
  187.4 3.6 %all-to-all-start.3 = ((bf16[4,144,1024]{2,1,0:T(8,128)(2,1)}), bf16[4,144,1024]{2,1,0:T(8,128)(2,1)S(1)}, u32[]{:S(2)}, u32[]{:S(2)}) async-start(bf16[4,144,1024]{2,1,0:T(8,128)(2,1)} %bitcast.78), calls=%async_computation.3 | async-start | bytes 2359296 | tf_op jit(solution)/shard_map/all_to_all | solution.py:259
  191.0 142.6 %all-reduce.2.cloned.1.call-done = f32[33,1024]{1,0:T(8,128)} async-done(((f32[33,1024]{1,0:T(8,128)}), f32[33,1024]{1,0:T(8,128)}) %all-reduce.2.cloned.1.call-update) | async-done | bytes 135184 | tf_op jit(solution)/shard_map/psum | solution.py:308
  333.6 1.6 slice.17
  335.2 1.4 slice.18
  336.6 0.0 all-to-all-done.3
  336.6 2.0 add_convert_fusion
  338.7 2.8 bitcast_convert_fusion.1
  341.5 2.8 bitcast_convert_fusion
  (24 shorter events, 0.1 us)
Async XLA Ops:
  8.0 13.4 %copy-start = (s32[2]{0:T(128)S(1)}, s32[2]{0:T(128)}, u32[]{:S(2)}) copy-start(s32[2]{0:T(128)} %len_ref.3) | copy-start | bytes 28
  8.0 13.4 %copy-start.4 = (f32[1024]{0:T(1024)S(1)}, f32[1024]{0:T(1024)}, u32[]{:S(2)}) copy-start(f32[1024]{0:T(1024)} %param.13) | copy-start | bytes 12292
  8.0 13.3 %copy-start.5 = (f32[1024]{0:T(1024)S(1)}, f32[1024]{0:T(1024)}, u32[]{:S(2)}) copy-start(f32[1024]{0:T(1024)} %param.14) | copy-start | bytes 12292
  8.0 13.3 %copy-start.3 = (f32[31,1024]{1,0:T(8,128)S(1)}, f32[31,1024]{1,0:T(8,128)}, u32[]{:S(2)}) copy-start(f32[31,1024]{1,0:T(8,128)} %taps_ref.3) | copy-start | bytes 380932
  8.0 13.3 %copy-start.1 = (bf16[512,1024]{1,0:T(8,128)(2,1)S(1)}, bf16[512,1024]{1,0:T(8,128)(2,1)}, u32[]{:S(2)}) copy-start(bf16[512,1024]{1,0:T(8,128)(2,1)} %x_ref.3) | copy-start | bytes 3145732
  15.0 34.9 %all-to-all-start = ((bf16[4,144,1024]{2,1,0:T(8,128)(2,1)}), bf16[4,144,1024]{2,1,0:T(8,128)(2,1)S(1)}, u32[]{:S(2)}, u32[]{:S(2)}) async-start(bf16[4,144,1024]{2,1,0:T(8,128)(2,1)} %bitcast.6), calls=%async_computation | async-start | bytes 2359296 | tf_op jit(solution)/shard_map/all_to_all | solution.py:259
  35.8 1.3 copy-start.6
  37.1 1.3 copy-start.9
  81.4 23.1 %slice-start = ((s8[8388608]{0:T(1024)(128)(4,1)}), s8[4194304]{0:T(1024)(128)(4,1)S(1)}, s32[]{:S(2)}) async-start(s8[8388608]{0:T(1024)(128)(4,1)} %bitcast.85), calls=%async_computation.9 | async-start | bytes 8388608
  93.6 11.0 %slice-start.1 = ((s8[8388608]{0:T(1024)(128)(4,1)}), s8[4194304]{0:T(1024)(128)(4,1)S(1)}, s32[]{:S(2)}) async-start(s8[8388608]{0:T(1024)(128)(4,1)} %bitcast.85), calls=%async_computation.10 | async-start | bytes 8388608
  104.6 6.2 %copy-start.11 = (bf16[576,4096]{1,0:T(8,128)(2,1)}, bf16[576,4096]{1,0:T(8,128)(2,1)S(1)}, u32[]{:S(2)}) copy-start(bf16[576,4096]{1,0:T(8,128)(2,1)S(1)} %multiply_convert_fusion) | copy-start | bytes 14155780
  110.7 32.0 %all-to-all-start.2 = ((bf16[4,144,1024]{2,1,0:T(8,128)(2,1)}), bf16[4,144,1024]{2,1,0:T(8,128)(2,1)}, u32[]{:S(2)}, u32[]{:S(2)}) async-start(bf16[4,144,1024]{2,1,0:T(8,128)(2,1)} %bitcast.12), calls=%async_computation.2 | async-start | bytes 2359296 | tf_op jit(solution)/shard_map/all_to_all | solution.py:259
  115.0 218.6 %all-reduce.2.cloned.1.call-start = ((), (), s32[]{:S(2)}) async-start(), calls=%async_computation.8 | async-start | bytes 327680 | tf_op jit(solution)/shard_map/psum | solution.py:308
  126.6 18.4 %copy-start.2 = (bf16[512,1024]{1,0:T(8,128)(2,1)S(1)}, bf16[512,1024]{1,0:T(8,128)(2,1)}, u32[]{:S(2)}) copy-start(bf16[512,1024]{1,0:T(8,128)(2,1)} %grad_ref.1) | copy-start | bytes 3145732
  145.0 1.6 copy-start.7
  146.6 1.6 copy-start.10
  176.5 162.2 %reduce-scatter.3.cloned.1.call-start = ((), (), s32[]{:S(2)}) async-start(), calls=%async_computation.6 | async-start | bytes 9437184 | tf_op jit(solution)/shard_map/reduce_scatter | solution.py:297
  177.0 164.5 %reduce-scatter.5.cloned.1.call-start = ((), (), s32[]{:S(2)}) async-start(), calls=%async_computation.7 | async-start | bytes 9437184 | tf_op jit(solution)/shard_map/reduce_scatter | solution.py:298
  177.6 159.0 %copy-start.8 = (f32[512,1024]{1,0:T(8,128)S(1)}, f32[512,1024]{1,0:T(8,128)}, u32[]{:S(2)}) copy-start(f32[512,1024]{1,0:T(8,128)} %copy-done.6) | copy-start | bytes 6291460
  187.4 149.2 %all-to-all-start.3 = ((bf16[4,144,1024]{2,1,0:T(8,128)(2,1)}), bf16[4,144,1024]{2,1,0:T(8,128)(2,1)S(1)}, u32[]{:S(2)}, u32[]{:S(2)}) async-start(bf16[4,144,1024]{2,1,0:T(8,128)(2,1)} %bitcast.78), calls=%async_computation.3 | async-start | bytes 2359296 | tf_op jit(solution)/shard_map/all_to_all | solution.py:259
Sparse Core Ops, SparseCore 0:
  176.6 157.0 all-reduce.1
Sparse Core Ops, SparseCore 1:
  180.4 70.4 reduce-scatter.2
  254.6 71.3 reduce-scatter.4

commit v2 on v1

--- a/solution.py
+++ b/solution.py
@@ -259,6 +259,27 @@
     return lax.all_to_all(rows, "expert", split_axis=0, concat_axis=0, tiled=True)
 
 
+def column_part(matrix, place, part):
+    return lax.dynamic_slice_in_dim(matrix, place * part, part, axis=1)
+
+
+def sum_over_dp(part_of, flip):
+    count = lax.axis_size("dp")
+    me = lax.axis_index("dp")
+    steps = [1 << bit for bit in range(count.bit_length() - 1)]
+    if flip:
+        steps = steps[:1] + steps[:0:-1]
+    order = sorted(range(count), key=lambda piece: -(piece & 1))
+    pieces = {piece: part_of(me ^ piece) for piece in order}
+    for bit in steps:
+        pairs = [(device, device ^ bit) for device in range(count)]
+        arrived = {
+            piece ^ bit: lax.ppermute(pieces[piece].astype(BF16), "dp", pairs) for piece in pieces if piece & bit
+        }
+        pieces = {piece: pieces[piece] + arrived[piece].astype(F32) for piece in arrived}
+    return pieces[0]
+
+
 def shards(frames, lengths, expert_ids, conv_kernel, conv_gain, ffn_gain, w_in, w_out, out_grad):
     utt_count = lengths.shape[0]
     frame_count, width = frames.shape
@@ -292,11 +313,9 @@
     back_rows = times_transpose(pre_grad, weights_in).astype(BF16)
     ret_back = exchange(back_rows)
     pre_grad, back_rows = lax.optimization_barrier((pre_grad, back_rows))
-    full_in = contract_rows(routed_in, pre_grad).astype(BF16)
-    full_out = contract_rows(hidden, grad_rows).astype(BF16)
-    grad_in = lax.psum_scatter(full_in, "dp", scatter_dimension=1, tiled=True).astype(F32)
-    grad_out = lax.psum_scatter(full_out, "dp", scatter_dimension=0, tiled=True).astype(F32)
-    hidden, full_in, full_out, ret_back = lax.optimization_barrier((hidden, full_in, full_out, ret_back))
+    part = w_in.shape[2] // lax.axis_size("dp")
+    grad_in = sum_over_dp(lambda place: contract_rows(routed_in, column_part(pre_grad, place, part)), False)
+    grad_out = sum_over_dp(lambda place: contract_rows(column_part(hidden, place, part), grad_rows), True)
     out_rows = jnp.dot(hidden, weights_out, preferred_element_type=F32).astype(BF16)
     ret_out = exchange(out_rows)
 

time: 354 us -> 378 us (1.068)
  matrix products: 70.9 us -> 103 us
  blocking collectives: 31.5 us -> 0 us
  starting transfers between devices: 14.5 us -> 28.8 us
  other arithmetic: 9.34 us -> 18.1 us
  waiting for transfers between devices: 158 us -> 164 us
  local copies, waits for them, and re-layouts: 9.1 us -> 4.64 us
    dot_general x4 -> x18, matrix products: 27 us -> 59.7 us  [contract_rows(): lax.dot_general(left_rows, right_rows, (((0,), (0,)), ((), ())), preferre...]
    all_to_all x1 -> x0, blocking collectives: 31.5 us -> none  [exchange(): lax.all_to_all(rows, 'expert', split_axis=0, concat_axis=0, tiled=True)]
    all_to_all x3 -> x4, waiting for transfers between devices: 14.3 us -> 39.1 us  [exchange(): lax.all_to_all(rows, 'expert', split_axis=0, concat_axis=0, tiled=True)]
    psum x1, waiting for transfers between devices: 143 us -> 120 us  [shards(): sums = lax.psum(sums, ('dp', 'expert'))]
    ppermute x0 -> x14, starting transfers between devices: none -> 8.95 us  [sum_over_dp(): lax.ppermute(pieces[piece].astype(BF16), 'dp', pairs)]
    convert_element_type x0 -> x2, other arithmetic: none -> 6.15 us  [sum_over_dp(): pieces[piece].astype(BF16)]
    all_to_all x3 -> x4, starting transfers between devices: 14.2 us -> 19.9 us  [exchange(): lax.all_to_all(rows, 'expert', split_axis=0, concat_axis=0, tiled=True)]
    ppermute x0 -> x14, waiting for transfers between devices: none -> 5.13 us  [sum_over_dp(): lax.ppermute(pieces[piece].astype(BF16), 'dp', pairs)]
  transfers between devices with their start and end apart: 6 -> 19, of which waited for: 3 -> 4; matrix products, arithmetic and copies ran while one was open for 12% -> 14% of each run, Pallas kernels for 4% -> 11%
where the time goes in v2:
time: 378 us; the launch traced here: 376 us
  waiting for transfers between devices  164 us (43%)
  matrix products  103 us (27%)
  Pallas kernels  42.8 us (11%)
  starting transfers between devices  28.8 us (8%)
  other arithmetic  18.1 us (5%)
  between operations  14.3 us (4%)
  local copies, waits for them, and re-layouts  4.64 us (1%)
    psum x1, waiting for transfers between devices, shards(): sums = lax.psum(sums, ('dp', 'expert'))  120 us
    dot_general x18, matrix products, contract_rows(): lax.dot_general(left_rows, right_rows, (((0,), (0,)), ((), ())), preferre...  59.7 us
    all_to_all x4, waiting for transfers between devices, exchange(): lax.all_to_all(rows, 'expert', split_axis=0, concat_axis=0, tiled=True)  39.1 us
    pallas_call x1, Pallas kernels, conv_backward(): pl.pallas_call(conv_backward_kernel, grid=(utt_count,), out_shape=[jax.Sh...  28.4 us
    all_to_all x4, starting transfers between devices, exchange(): lax.all_to_all(rows, 'expert', split_axis=0, concat_axis=0, tiled=True)  19.9 us
    dot_general x2, matrix products, times_transpose(): lax.dot_general(left_rows, matrix, (((1,), (1,)), ((), ())), preferred_el...  16.9 us
    pallas_call x1, Pallas kernels, conv_forward(): pl.pallas_call(conv_forward_kernel, grid=(utt_count,), out_shape=[jax.Sha...  14.4 us
    dot_general x1, matrix products, shards(): pre_act = jnp.dot(routed_in, weights_in, preferred_element_type=F32)  10.7 us
  transfers between devices with their start and end apart: 19, of which 4 were waited for; matrix products, arithmetic and copies ran while one was open for 14% of the time, Pallas kernels for 11%

profile of v2, /device:TPU:0, one launch (start us, length us, event | category | flops | bytes accessed | tf_op | source)
XLA Modules:
  0.0 375.6 jit_solution(17096785084735389350)
XLA Ops:
  7.2 0.7 fusion.71
  8.6 1.2 reduce-window.6
  10.3 0.7 add_select_fusion
  11.1 3.2 convolution_convert_fusion
  14.2 6.3 %all-to-all-start = ((bf16[4,144,1024]{2,1,0:T(8,128)(2,1)}), bf16[4,144,1024]{2,1,0:T(8,128)(2,1)}, u32[]{:S(2)}, u32[]{:S(2)}) async-start(bf16[4,144,1024]{2,1,0:T(8,128)(2,1)} %bitcast.6), calls=%async_computation | async-start | bytes 2359296 | tf_op jit(solution)/shard_map/all_to_all | solution.py:259
  20.6 14.4 %conv_forward.1 = (f32[512,1024]{1,0:T(8,128)S(1)}, f32[512,1024]{1,0:T(8,128)S(1)}, bf16[512,1024]{1,0:T(8,128)(2,1)S(1)}) custom-call(s32[2]{0:T(128)S(1)} %copy-done, bf16[512,1024]{1,0:T(8,128)(2,1)S(1)} %copy-done.1, f32[31,1024]{1,0:T(8,128)S(1)} %copy-done.3, f32[1,1024]{1,0:T(1,128)S(1)} %bitcast.79, f32[1,1024]{1,0:T(1,128)S(1)} %bitcast.81), custom_call_target="tpu_custom_call" | custom-call | flops 8589934592 | bytes 41943040 | tf_op jit(solution)/shard_map/conv_forward/pallas_call | solution.py:199
  35.0 1.3 copy-done.6
  36.3 1.8 convolution_convert_fusion.1
  38.1 11.1 %all-to-all-done = bf16[4,144,1024]{2,1,0:T(8,128)(2,1)} async-done(((bf16[4,144,1024]{2,1,0:T(8,128)(2,1)}), bf16[4,144,1024]{2,1,0:T(8,128)(2,1)}, u32[]{:S(2)}, u32[]{:S(2)}) %all-to-all-start) | async-done | bytes 1179680 | tf_op jit(solution)/shard_map/all_to_all | solution.py:259
  49.2 4.3 %all-to-all-start.1 = ((bf16[4,144,1024]{2,1,0:T(8,128)(2,1)}), bf16[4,144,1024]{2,1,0:T(8,128)(2,1)}, u32[]{:S(2)}, u32[]{:S(2)}) async-start(bf16[4,144,1024]{2,1,0:T(8,128)(2,1)} %bitcast.84), calls=%async_computation.1 | async-start | bytes 2359296 | tf_op jit(solution)/shard_map/all_to_all | solution.py:259
  53.5 28.1 %all-to-all-done.1 = bf16[4,144,1024]{2,1,0:T(8,128)(2,1)} async-done(((bf16[4,144,1024]{2,1,0:T(8,128)(2,1)}), bf16[4,144,1024]{2,1,0:T(8,128)(2,1)}, u32[]{:S(2)}, u32[]{:S(2)}) %all-to-all-start.1) | async-done | bytes 1179680 | tf_op jit(solution)/shard_map/all_to_all | solution.py:259
  81.6 10.7 %multiply_convert_fusion.1 = (bf16[576,4096]{1,0:T(8,128)(2,1)S(1)}, f32[576,4096]{1,0:T(8,128)}) fusion(bf16[576,1024]{1,0:T(8,128)(2,1)} %bitcast.9, bf16[1,1024,4096]{2,1,0:T(8,128)(2,1)} %param.15), kind=kOutput, calls=%fused_computation.1 | convolution fusion | flops 4843634688 | bytes 23724032 | tf_op jit(solution)/shard_map/dot_general | solution.py:310
  92.3 10.4 %fusion.13 = bf16[576,1024]{1,0:T(8,128)(2,1)} fusion(bf16[576,4096]{1,0:T(8,128)(2,1)S(1)} %get-tuple-element.24, bf16[1,4096,1024]{2,1,0:T(8,128)(2,1)} %param.16), kind=kOutput, calls=%fused_computation.21 | convolution fusion | flops 4832428032 | bytes 14286848 | tf_op jit(solution)/shard_map/dot_general | solution.py:319
  102.7 10.8 %multiply_convert_fusion = bf16[576,4096]{1,0:T(8,128)(2,1)S(1)} fusion(f32[576,4096]{1,0:T(8,128)} %get-tuple-element.25, bf16[576,1024]{1,0:T(8,128)(2,1)} %bitcast.7, bf16[1,4096,1024]{2,1,0:T(8,128)(2,1)} %param.16), kind=kOutput, calls=%fused_computation | convolution fusion | flops 4853071872 | bytes 23724032 | tf_op jit(solution)/shard_map/dot_general | solution.py:255
  113.6 6.1 %fusion.10 = bf16[576,1024]{1,0:T(8,128)(2,1)} fusion(bf16[576,4096]{1,0:T(8,128)(2,1)S(1)} %multiply_convert_fusion, bf16[1,1024,4096]{2,1,0:T(8,128)(2,1)S(1)} %bitcast.92), kind=kOutput, calls=%fused_computation.20 | convolution fusion | flops 4832428032 | bytes 14286848 | tf_op jit(solution)/shard_map/dot_general | solution.py:255
  119.7 3.4 convolution_convert_fusion.2
  123.1 3.3 convolution_convert_fusion.6
  126.4 3.3 convolution_convert_fusion.7
  129.7 3.4 convolution_convert_fusion.4
  133.2 3.7 fusion.46
  136.8 3.8 %fusion.30 = f32[512,1024]{1,0:T(8,128)} fusion(bf16[576,1024]{1,0:T(8,128)(2,1)} %bitcast.7, bf16[576,4096]{1,0:T(8,128)(2,1)} %copy-done.15, s32[]{:T(128)S(6)} %select_n.53), kind=kOutput, calls=%fused_computation.44 | convolution fusion | flops 603979776 | bytes 3866628 | tf_op jit(solution)/shard_map/dot_general | solution.py:251
  140.7 4.5 %all-to-all-start.3 = ((bf16[4,144,1024]{2,1,0:T(8,128)(2,1)}), bf16[4,144,1024]{2,1,0:T(8,128)(2,1)}, u32[]{:S(2)}, u32[]{:S(2)}) async-start(bf16[4,144,1024]{2,1,0:T(8,128)(2,1)} %bitcast.85), calls=%async_computation.3 | async-start | bytes 2359296 | tf_op jit(solution)/shard_map/all_to_all | solution.py:259
  145.2 3.9 %fusion.38 = f32[1024,512]{1,0:T(8,128)} fusion(bf16[576,1024]{1,0:T(8,128)(2,1)} %bitcast.9, bf16[576,4096]{1,0:T(8,128)(2,1)} %copy-done.13, s32[]{:T(128)S(6)} %select_n.57), kind=kOutput, calls=%fused_computation.50 | convolution fusion | flops 603979776 | bytes 3866628 | tf_op jit(solution)/shard_map/dot_general | solution.py:251
  149.5 2.5 convolution_convert_fusion.8
  152.7 3.8 %fusion.22 = f32[512,1024]{1,0:T(8,128)} fusion(bf16[576,1024]{1,0:T(8,128)(2,1)} %bitcast.7, bf16[576,4096]{1,0:T(8,128)(2,1)} %copy-done.15, s32[]{:T(128)S(6)} %select_n.55), kind=kOutput, calls=%fused_computation.38 | convolution fusion | flops 603979776 | bytes 3866628 | tf_op jit(solution)/shard_map/dot_general | solution.py:251
  156.5 3.3 convolution_convert_fusion.9
  159.8 3.3 convolution_convert_fusion.5
  163.1 3.3 convolution_convert_fusion.3
  166.7 3.3 add_convert_fusion.4
  170.0 1.5 collective-permute-start.5
  171.5 3.3 add_convert_fusion.1
  174.8 1.5 collective-permute-start.12
  176.3 3.3 add_convert_fusion.5
  179.6 3.3 add_convert_fusion.2
  182.9 4.8 %all-to-all-start.2 = ((bf16[4,144,1024]{2,1,0:T(8,128)(2,1)}), bf16[4,144,1024]{2,1,0:T(8,128)(2,1)}, u32[]{:S(2)}, u32[]{:S(2)}) async-start(bf16[4,144,1024]{2,1,0:T(8,128)(2,1)} %bitcast.83), calls=%async_computation.2 | async-start | bytes 2359296 | tf_op jit(solution)/shard_map/all_to_all | solution.py:259
  187.6 2.4 convolution_convert_fusion.10.back_ref
  190.4 5.1 %collective-permute-done.5 = bf16[1024,512]{1,0:T(8,128)(2,1)} collective-permute-done((bf16[1024,512]{1,0:T(8,128)(2,1)}, bf16[1024,512]{1,0:T(8,128)(2,1)}, u32[]{:S(2)}, u32[]{:S(2)}) %collective-permute-start.5) | collective-permute-done | bytes 1048608 | tf_op jit(solution)/shard_map/ppermute | solution.py:277
  195.5 1.5 collective-permute-start.2
  197.0 3.1 add_convert_fusion.3
  200.1 1.6 collective-permute-start.9
  202.2 3.1 add_convert_fusion
  205.8 28.4 %conv_backward.1 = (bf16[512,1024]{1,0:T(8,128)(2,1)}, f32[33,1024]{1,0:T(8,128)}) custom-call(s32[2]{0:T(128)S(1)} %copy-done, bf16[512,1024]{1,0:T(8,128)(2,1)S(1)} %copy-done.1, f32[31,1024]{1,0:T(8,128)S(1)} %copy-done.3, f32[1,1024]{1,0:T(1,128)S(1)} %bitcast.80, f32[1,1024]{1,0:T(1,128)S(1)} %bitcast.82, f32[512,1024]{1,0:T(8,128)S(1)} %get-tuple-element.14.res_ref, ...), custom_call_target="tpu_custom_call" | custom-call | flops 8589934592 | bytes 83886080 | tf_op jit(solution)/shard_map/conv_backward/pallas_call | solution.py:223
  234.2 3.3 add_convert_fusion.6
  237.5 119.9 %all-reduce.2.cloned.1.call-done = f32[33,1024]{1,0:T(8,128)} async-done(((f32[33,1024]{1,0:T(8,128)}), f32[33,1024]{1,0:T(8,128)}) %all-reduce.2.cloned.1.call-update) | async-done | bytes 135184 | tf_op jit(solution)/shard_map/psum | solution.py:327
  357.4 1.6 slice.17
  358.9 1.4 slice.18
  360.4 4.5 %add_bitcast_fusion.1 = f32[1,1024,512]{2,1,0:T(8,128)} fusion(bf16[1024,512]{1,0:T(8,128)(2,1)} %collective-permute-done.6, bf16[1024,512]{1,0:T(8,128)(2,1)} %collective-permute-done.2, f32[1024,512]{1,0:T(8,128)} %fusion.46, bf16[1024,512]{1,0:T(8,128)(2,1)} %collective-permute-done), kind=kLoop, calls=%fused_computation.15 | loop fusion | flops 3145728 | bytes 7340032 | tf_op jit(solution)/shard_map/broadcast_in_dim | solution.py:328
  364.9 3.9 %add_bitcast_fusion = f32[1,512,1024]{2,1,0:T(8,128)} fusion(bf16[512,1024]{1,0:T(8,128)(2,1)} %collective-permute-done.13, bf16[512,1024]{1,0:T(8,128)(2,1)} %collective-permute-done.9, f32[512,1024]{1,0:T(8,128)S(1)} %copy-done.8, bf16[512,1024]{1,0:T(8,128)(2,1)} %collective-permute-done.7), kind=kLoop, calls=%fused_computation.11 | loop fusion | flops 3145728 | bytes 7340032 | tf_op jit(solution)/shard_map/broadcast_in_dim | solution.py:328
  (76 shorter events, 4.2 us)
Async XLA Ops:
  11.0 9.5 %copy-start = (s32[2]{0:T(128)S(1)}, s32[2]{0:T(128)}, u32[]{:S(2)}) copy-start(s32[2]{0:T(128)} %len_ref.3) | copy-start | bytes 28
  11.0 9.5 %copy-start.1 = (bf16[512,1024]{1,0:T(8,128)(2,1)S(1)}, bf16[512,1024]{1,0:T(8,128)(2,1)}, u32[]{:S(2)}) copy-start(bf16[512,1024]{1,0:T(8,128)(2,1)} %x_ref.3) | copy-start | bytes 3145732
  11.0 9.5 %copy-start.3 = (f32[31,1024]{1,0:T(8,128)S(1)}, f32[31,1024]{1,0:T(8,128)}, u32[]{:S(2)}) copy-start(f32[31,1024]{1,0:T(8,128)} %taps_ref.3) | copy-start | bytes 380932
  11.0 9.5 %copy-start.4 = (f32[1024]{0:T(1024)S(1)}, f32[1024]{0:T(1024)}, u32[]{:S(2)}) copy-start(f32[1024]{0:T(1024)} %param.13) | copy-start | bytes 12292
  11.1 9.5 %copy-start.5 = (f32[1024]{0:T(1024)S(1)}, f32[1024]{0:T(1024)}, u32[]{:S(2)}) copy-start(f32[1024]{0:T(1024)} %param.14) | copy-start | bytes 12292
  14.2 35.0 %all-to-all-start = ((bf16[4,144,1024]{2,1,0:T(8,128)(2,1)}), bf16[4,144,1024]{2,1,0:T(8,128)(2,1)}, u32[]{:S(2)}, u32[]{:S(2)}) async-start(bf16[4,144,1024]{2,1,0:T(8,128)(2,1)} %bitcast.6), calls=%async_computation | async-start | bytes 2359296 | tf_op jit(solution)/shard_map/all_to_all | solution.py:259
  35.0 1.3 copy-start.6
  49.2 32.4 %all-to-all-start.1 = ((bf16[4,144,1024]{2,1,0:T(8,128)(2,1)}), bf16[4,144,1024]{2,1,0:T(8,128)(2,1)}, u32[]{:S(2)}, u32[]{:S(2)}) async-start(bf16[4,144,1024]{2,1,0:T(8,128)(2,1)} %bitcast.84), calls=%async_computation.1 | async-start | bytes 2359296 | tf_op jit(solution)/shard_map/all_to_all | solution.py:259
  92.3 10.4 %copy-start.15 = (bf16[576,4096]{1,0:T(8,128)(2,1)}, bf16[576,4096]{1,0:T(8,128)(2,1)S(1)}, u32[]{:S(2)}) copy-start(bf16[576,4096]{1,0:T(8,128)(2,1)S(1)} %get-tuple-element.24) | copy-start | bytes 14155780
  92.3 21.2 %slice-start = ((s8[8388608]{0:T(1024)(128)(4,1)}), s8[4194304]{0:T(1024)(128)(4,1)S(1)}, s32[]{:S(2)}) async-start(s8[8388608]{0:T(1024)(128)(4,1)} %bitcast.91), calls=%async_computation.5 | async-start | bytes 8388608
  102.7 10.8 %slice-start.1 = ((s8[8388608]{0:T(1024)(128)(4,1)}), s8[4194304]{0:T(1024)(128)(4,1)S(1)}, s32[]{:S(2)}) async-start(s8[8388608]{0:T(1024)(128)(4,1)} %bitcast.91), calls=%async_computation.6 | async-start | bytes 8388608
  113.6 19.6 %copy-start.13 = (bf16[576,4096]{1,0:T(8,128)(2,1)}, bf16[576,4096]{1,0:T(8,128)(2,1)S(1)}, u32[]{:S(2)}) copy-start(bf16[576,4096]{1,0:T(8,128)(2,1)S(1)} %multiply_convert_fusion) | copy-start | bytes 14155780
  140.7 42.2 %all-to-all-start.3 = ((bf16[4,144,1024]{2,1,0:T(8,128)(2,1)}), bf16[4,144,1024]{2,1,0:T(8,128)(2,1)}, u32[]{:S(2)}, u32[]{:S(2)}) async-start(bf16[4,144,1024]{2,1,0:T(8,128)(2,1)} %bitcast.85), calls=%async_computation.3 | async-start | bytes 2359296 | tf_op jit(solution)/shard_map/all_to_all | solution.py:259
  145.2 4.4 %copy-start.14 = (bf16[576,4096]{1,0:T(8,128)(2,1)S(1)}, bf16[576,4096]{1,0:T(8,128)(2,1)}, u32[]{:S(2)}) copy-start(bf16[576,4096]{1,0:T(8,128)(2,1)} %copy-done.13) | copy-start | bytes 14155780
  145.2 21.2 %collective-permute-start.4 = (bf16[1024,512]{1,0:T(8,128)(2,1)}, bf16[1024,512]{1,0:T(8,128)(2,1)S(1)}, u32[]{:S(2)}, u32[]{:S(2)}) collective-permute-start(bf16[1024,512]{1,0:T(8,128)(2,1)} %convolution_convert_fusion.6), channel_id=1, source_target_pairs={{0,4},{4,0},{8,12},{12,8},{16,20},{20,16},{24,28},{28,24},{1,5},{5... | collective-permute-start | bytes 3145736 | tf_op jit(solution)/shard_map/ppermute | solution.py:277
  149.2 3.1 copy-start.12
  149.2 3.4 copy-start.11
  149.2 40.9 %collective-permute-start.3 = (bf16[1024,512]{1,0:T(8,128)(2,1)}, bf16[1024,512]{1,0:T(8,128)(2,1)}, u32[]{:S(2)}, u32[]{:S(2)}) collective-permute-start(bf16[1024,512]{1,0:T(8,128)(2,1)} %convolution_convert_fusion.7), channel_id=1, source_target_pairs={{0,4},{4,0},{8,12},{12,8},{16,20},{20,16},{24,28},{28,24},{1,5},{5... | collective-permute-start | bytes 3145736 | tf_op jit(solution)/shard_map/ppermute | solution.py:277
  149.5 10.3 %slice-start.2 = ((s8[4718592]{0:T(1024)(128)(4,1)}), s8[4194304]{0:T(1024)(128)(4,1)S(1)}, s32[]{:S(2)}) async-start(s8[4718592]{0:T(1024)(128)(4,1)} %bitcast.93), calls=%async_computation.7 | async-start | bytes 8388608
  152.0 7.9 %slice-start.3 = ((s8[4718592]{0:T(1024)(128)(4,1)}), s8[524288]{0:T(1024)(128)(4,1)S(1)}, s32[]{:S(2)}) async-start(s8[4718592]{0:T(1024)(128)(4,1)} %bitcast.93), calls=%async_computation.8 | async-start | bytes 1048576
  152.0 22.8 %collective-permute-start.1 = (bf16[1024,512]{1,0:T(8,128)(2,1)S(1)}, bf16[1024,512]{1,0:T(8,128)(2,1)S(1)}, u32[]{:S(2)}, u32[]{:S(2)}) collective-permute-start(bf16[1024,512]{1,0:T(8,128)(2,1)S(1)} %convolution_convert_fusion.8), channel_id=1, source_target_pairs={{0,4},{4,0},{8,12},{12,8},{16,20},{20,16},{24,28},{28,24},{1,5},{5... | collective-permute-start | bytes 3145736 | tf_op jit(solution)/shard_map/ppermute | solution.py:277
  152.2 17.8 %collective-permute-start.11 = (bf16[512,1024]{1,0:T(8,128)(2,1)S(1)}, bf16[512,1024]{1,0:T(8,128)(2,1)S(1)}, u32[]{:S(2)}, u32[]{:S(2)}) collective-permute-start(bf16[512,1024]{1,0:T(8,128)(2,1)S(1)} %copy-done.12), channel_id=1, source_target_pairs={{0,4},{4,0},{8,12},{12,8},{16,20},{20,16},{24,28},{28,24},{1,5},{5... | collective-permute-start | bytes 3145736 | tf_op jit(solution)/shard_map/ppermute | solution.py:277
  152.6 27.0 %collective-permute-start.8 = (bf16[512,1024]{1,0:T(8,128)(2,1)S(1)}, bf16[512,1024]{1,0:T(8,128)(2,1)S(1)}, u32[]{:S(2)}, u32[]{:S(2)}) collective-permute-start(bf16[512,1024]{1,0:T(8,128)(2,1)S(1)} %copy-done.11), channel_id=1, source_target_pairs={{0,4},{4,0},{8,12},{12,8},{16,20},{20,16},{24,28},{28,24},{1,5},{5... | collective-permute-start | bytes 3145736 | tf_op jit(solution)/shard_map/ppermute | solution.py:277
  166.3 33.7 %collective-permute-start.10 = (bf16[512,1024]{1,0:T(8,128)(2,1)}, bf16[512,1024]{1,0:T(8,128)(2,1)}, u32[]{:S(2)}, u32[]{:S(2)}) collective-permute-start(bf16[512,1024]{1,0:T(8,128)(2,1)} %convolution_convert_fusion.3), channel_id=1, source_target_pairs={{0,4},{4,0},{8,12},{12,8},{16,20},{20,16},{24,28},{28,24},{1,5},{5... | collective-permute-start | bytes 3145736 | tf_op jit(solution)/shard_map/ppermute | solution.py:277
  170.0 25.5 %collective-permute-start.5 = (bf16[1024,512]{1,0:T(8,128)(2,1)}, bf16[1024,512]{1,0:T(8,128)(2,1)}, u32[]{:S(2)}, u32[]{:S(2)}) collective-permute-start(bf16[1024,512]{1,0:T(8,128)(2,1)} %add_convert_fusion.4), channel_id=1, source_target_pairs={{0,8},{4,12},{8,0},{12,4},{16,24},{20,28},{24,16},{28,20},{1,9},{5... | collective-permute-start | bytes 3145736 | tf_op jit(solution)/shard_map/ppermute | solution.py:277
  174.8 26.9 %collective-permute-start.12 = (bf16[512,1024]{1,0:T(8,128)(2,1)}, bf16[512,1024]{1,0:T(8,128)(2,1)}, u32[]{:S(2)}, u32[]{:S(2)}) collective-permute-start(bf16[512,1024]{1,0:T(8,128)(2,1)} %add_convert_fusion.1), channel_id=1, source_target_pairs={{0,16},{4,20},{8,24},{12,28},{16,0},{20,4},{24,8},{28,12},{1,17},{... | collective-permute-start | bytes 3145736 | tf_op jit(solution)/shard_map/ppermute | solution.py:277
  179.6 25.7 %collective-permute-start = (bf16[1024,512]{1,0:T(8,128)(2,1)}, bf16[1024,512]{1,0:T(8,128)(2,1)}, u32[]{:S(2)}, u32[]{:S(2)}) collective-permute-start(bf16[1024,512]{1,0:T(8,128)(2,1)} %convolution_convert_fusion.9), channel_id=1, source_target_pairs={{0,4},{4,0},{8,12},{12,8},{16,20},{20,16},{24,28},{28,24},{1,5},{5... | collective-permute-start | bytes 3145736 | tf_op jit(solution)/shard_map/ppermute | solution.py:277
  182.9 51.3 %all-to-all-start.2 = ((bf16[4,144,1024]{2,1,0:T(8,128)(2,1)}), bf16[4,144,1024]{2,1,0:T(8,128)(2,1)}, u32[]{:S(2)}, u32[]{:S(2)}) async-start(bf16[4,144,1024]{2,1,0:T(8,128)(2,1)} %bitcast.83), calls=%async_computation.2 | async-start | bytes 2359296 | tf_op jit(solution)/shard_map/all_to_all | solution.py:259
  187.6 169.7 %all-reduce.2.cloned.1.call-start = ((), (), s32[]{:S(2)}) async-start(), calls=%async_computation.4 | async-start | bytes 327680 | tf_op jit(solution)/shard_map/psum | solution.py:327
  187.6 9.4 %copy-start.10 = (f32[1024,512]{1,0:T(8,128)S(1)}, f32[1024,512]{1,0:T(8,128)}, u32[]{:S(2)}) copy-start(f32[1024,512]{1,0:T(8,128)} %fusion.38) | copy-start | bytes 6291460
  190.1 12.1 %copy-start.9 = (f32[512,1024]{1,0:T(8,128)S(1)}, f32[512,1024]{1,0:T(8,128)}, u32[]{:S(2)}) copy-start(f32[512,1024]{1,0:T(8,128)} %fusion.22) | copy-start | bytes 6291460
  190.1 174.8 %collective-permute-start.7 = (bf16[512,1024]{1,0:T(8,128)(2,1)}, bf16[512,1024]{1,0:T(8,128)(2,1)}, u32[]{:S(2)}, u32[]{:S(2)}) collective-permute-start(bf16[512,1024]{1,0:T(8,128)(2,1)} %convolution_convert_fusion.5), channel_id=1, source_target_pairs={{0,4},{4,0},{8,12},{12,8},{16,20},{20,16},{24,28},{28,24},{1,5},{5... | collective-permute-start | bytes 3145736 | tf_op jit(solution)/shard_map/ppermute | solution.py:277
  195.5 164.9 %collective-permute-start.2 = (bf16[1024,512]{1,0:T(8,128)(2,1)}, bf16[1024,512]{1,0:T(8,128)(2,1)}, u32[]{:S(2)}, u32[]{:S(2)}) collective-permute-start(bf16[1024,512]{1,0:T(8,128)(2,1)} %add_convert_fusion.5), channel_id=1, source_target_pairs={{0,8},{4,12},{8,0},{12,4},{16,24},{20,28},{24,16},{28,20},{1,9},{5... | collective-permute-start | bytes 3145736 | tf_op jit(solution)/shard_map/ppermute | solution.py:277
  200.1 5.7 %copy-start.2 = (bf16[512,1024]{1,0:T(8,128)(2,1)S(1)}, bf16[512,1024]{1,0:T(8,128)(2,1)}, u32[]{:S(2)}) copy-start(bf16[512,1024]{1,0:T(8,128)(2,1)} %grad_ref.1) | copy-start | bytes 3145732
  200.1 5.7 %copy-start.7 = (f32[512,1024]{1,0:T(8,128)S(1)}, f32[512,1024]{1,0:T(8,128)}, u32[]{:S(2)}) copy-start(f32[512,1024]{1,0:T(8,128)} %copy-done.6) | copy-start | bytes 6291460
  200.1 164.8 %collective-permute-start.9 = (bf16[512,1024]{1,0:T(8,128)(2,1)}, bf16[512,1024]{1,0:T(8,128)(2,1)}, u32[]{:S(2)}, u32[]{:S(2)}) collective-permute-start(bf16[512,1024]{1,0:T(8,128)(2,1)} %add_convert_fusion.2), channel_id=1, source_target_pairs={{0,16},{4,20},{8,24},{12,28},{16,0},{20,4},{24,8},{28,12},{1,17},{... | collective-permute-start | bytes 3145736 | tf_op jit(solution)/shard_map/ppermute | solution.py:277
  201.7 158.7 %collective-permute-start.6 = (bf16[1024,512]{1,0:T(8,128)(2,1)}, bf16[1024,512]{1,0:T(8,128)(2,1)}, u32[]{:S(2)}, u32[]{:S(2)}) collective-permute-start(bf16[1024,512]{1,0:T(8,128)(2,1)} %add_convert_fusion.3), channel_id=1, source_target_pairs={{0,16},{4,20},{8,24},{12,28},{16,0},{20,4},{24,8},{28,12},{1,17},{... | collective-permute-start | bytes 3145736 | tf_op jit(solution)/shard_map/ppermute | solution.py:277
  205.3 159.6 %collective-permute-start.13 = (bf16[512,1024]{1,0:T(8,128)(2,1)}, bf16[512,1024]{1,0:T(8,128)(2,1)}, u32[]{:S(2)}, u32[]{:S(2)}) collective-permute-start(bf16[512,1024]{1,0:T(8,128)(2,1)} %add_convert_fusion), channel_id=1, source_target_pairs={{0,8},{4,12},{8,0},{12,4},{16,24},{20,28},{24,16},{28,20},{1,9},{5... | collective-permute-start | bytes 3145736 | tf_op jit(solution)/shard_map/ppermute | solution.py:277
  360.4 4.5 %copy-start.8 = (f32[512,1024]{1,0:T(8,128)S(1)}, f32[512,1024]{1,0:T(8,128)}, u32[]{:S(2)}) copy-start(f32[512,1024]{1,0:T(8,128)} %fusion.30) | copy-start | bytes 6291460
Sparse Core Ops, SparseCore 0:
  234.3 123.0 all-reduce.1

commit v3 on v2

--- a/solution.py
+++ b/solution.py
@@ -324,8 +324,8 @@
         frames, lengths, conv_kernel, gain, ffn, residual, conv_out, expert_back, out_grad
     )
     block_out = (residual + contract_rows(placing, ret_out)).astype(BF16)
-    sums = lax.psum(sums, ("dp", "expert"))
-    return (block_out, frames_grad, grad_in[None], grad_out[None], sums[:taps], sums[taps:])
+    kernel_grad, gain_grads = lax.psum((sums[:taps], sums[taps:]), ("dp", "expert"))
+    return (block_out, frames_grad, grad_in[None], grad_out[None], kernel_grad, gain_grads)
 
 
 def solution(mesh):

time: 378 us -> 368 us (0.974)
  waiting for transfers between devices: 164 us -> 110 us
  blocking collectives: 0 us -> 46.8 us
    psum x1, waiting for transfers between devices: 120 us -> 65.7 us  [shards(): lax.psum((sums[:taps], sums[taps:]), ('dp', 'expert'))]
    psum x0 -> x1, blocking collectives: none -> 46.8 us  [shards(): lax.psum((sums[:taps], sums[taps:]), ('dp', 'expert'))]
  transfers between devices with their start and end apart: 19 -> 19, of which waited for: 4 -> 4; matrix products, arithmetic and copies ran while one was open for 14% -> 15% of each run, Pallas kernels for 11% -> 12%
where the time goes in v3:
time: 368 us; the launch traced here: 367 us
  waiting for transfers between devices  110 us (30%)
  matrix products  103 us (28%)
  blocking collectives  46.8 us (13%)
  Pallas kernels  42.4 us (12%)
  starting transfers between devices  28.8 us (8%)
  other arithmetic  17.5 us (5%)
  between operations  14.3 us (4%)
  local copies, waits for them, and re-layouts  3.88 us (1%)
    psum x1, waiting for transfers between devices, shards(): lax.psum((sums[:taps], sums[taps:]), ('dp', 'expert'))  65.7 us
    dot_general x18, matrix products, contract_rows(): lax.dot_general(left_rows, right_rows, (((0,), (0,)), ((), ())), preferre...  60 us
    psum x1, blocking collectives, shards(): lax.psum((sums[:taps], sums[taps:]), ('dp', 'expert'))  46.8 us
    all_to_all x4, waiting for transfers between devices, exchange(): lax.all_to_all(rows, 'expert', split_axis=0, concat_axis=0, tiled=True)  39.3 us
    pallas_call x1, Pallas kernels, conv_backward(): pl.pallas_call(conv_backward_kernel, grid=(utt_count,), out_shape=[jax.Sh...  28.2 us
    all_to_all x4, starting transfers between devices, exchange(): lax.all_to_all(rows, 'expert', split_axis=0, concat_axis=0, tiled=True)  19.9 us
    dot_general x2, matrix products, times_transpose(): lax.dot_general(left_rows, matrix, (((1,), (1,)), ((), ())), preferred_el...  16.9 us
    pallas_call x1, Pallas kernels, conv_forward(): pl.pallas_call(conv_forward_kernel, grid=(utt_count,), out_shape=[jax.Sha...  14.2 us
  transfers between devices with their start and end apart: 19, of which 4 were waited for; matrix products, arithmetic and copies ran while one was open for 15% of the time, Pallas kernels for 12%

profile of v3, /device:TPU:0, one launch (start us, length us, event | category | flops | bytes accessed | tf_op | source)
XLA Modules:
  0.0 367.0 jit_solution(6420622696540173248)
XLA Ops:
  7.2 0.7 fusion.71
  8.6 1.2 reduce-window.6
  10.3 0.7 add_select_fusion
  11.1 3.1 convolution_convert_fusion
  14.2 6.3 %all-to-all-start = ((bf16[4,144,1024]{2,1,0:T(8,128)(2,1)}), bf16[4,144,1024]{2,1,0:T(8,128)(2,1)}, u32[]{:S(2)}, u32[]{:S(2)}) async-start(bf16[4,144,1024]{2,1,0:T(8,128)(2,1)} %bitcast.6), calls=%async_computation | async-start | bytes 2359296 | tf_op jit(solution)/shard_map/all_to_all | solution.py:259
  20.6 14.2 %conv_forward.1 = (f32[512,1024]{1,0:T(8,128)S(1)}, f32[512,1024]{1,0:T(8,128)S(1)}, bf16[512,1024]{1,0:T(8,128)(2,1)S(1)}) custom-call(s32[2]{0:T(128)S(1)} %copy-done, bf16[512,1024]{1,0:T(8,128)(2,1)S(1)} %copy-done.1, f32[31,1024]{1,0:T(8,128)S(1)} %copy-done.3, f32[1,1024]{1,0:T(1,128)S(1)} %bitcast.79, f32[1,1024]{1,0:T(1,128)S(1)} %bitcast.81), custom_call_target="tpu_custom_call" | custom-call | flops 8589934592 | bytes 41943040 | tf_op jit(solution)/shard_map/conv_forward/pallas_call | solution.py:199
  34.8 1.3 copy-done.6
  36.1 1.8 convolution_convert_fusion.1
  37.9 11.3 %all-to-all-done = bf16[4,144,1024]{2,1,0:T(8,128)(2,1)} async-done(((bf16[4,144,1024]{2,1,0:T(8,128)(2,1)}), bf16[4,144,1024]{2,1,0:T(8,128)(2,1)}, u32[]{:S(2)}, u32[]{:S(2)}) %all-to-all-start) | async-done | bytes 1179680 | tf_op jit(solution)/shard_map/all_to_all | solution.py:259
  49.2 4.3 %all-to-all-start.1 = ((bf16[4,144,1024]{2,1,0:T(8,128)(2,1)}), bf16[4,144,1024]{2,1,0:T(8,128)(2,1)}, u32[]{:S(2)}, u32[]{:S(2)}) async-start(bf16[4,144,1024]{2,1,0:T(8,128)(2,1)} %bitcast.84), calls=%async_computation.1 | async-start | bytes 2359296 | tf_op jit(solution)/shard_map/all_to_all | solution.py:259
  53.5 28.1 %all-to-all-done.1 = bf16[4,144,1024]{2,1,0:T(8,128)(2,1)} async-done(((bf16[4,144,1024]{2,1,0:T(8,128)(2,1)}), bf16[4,144,1024]{2,1,0:T(8,128)(2,1)}, u32[]{:S(2)}, u32[]{:S(2)}) %all-to-all-start.1) | async-done | bytes 1179680 | tf_op jit(solution)/shard_map/all_to_all | solution.py:259
  81.5 10.8 %multiply_convert_fusion.1 = (bf16[576,4096]{1,0:T(8,128)(2,1)S(1)}, f32[576,4096]{1,0:T(8,128)}) fusion(bf16[576,1024]{1,0:T(8,128)(2,1)} %bitcast.9, bf16[1,1024,4096]{2,1,0:T(8,128)(2,1)} %param.15), kind=kOutput, calls=%fused_computation.1 | convolution fusion | flops 4843634688 | bytes 23724032 | tf_op jit(solution)/shard_map/dot_general | solution.py:310
  92.3 10.4 %fusion.13 = bf16[576,1024]{1,0:T(8,128)(2,1)} fusion(bf16[576,4096]{1,0:T(8,128)(2,1)S(1)} %get-tuple-element.24, bf16[1,4096,1024]{2,1,0:T(8,128)(2,1)} %param.16), kind=kOutput, calls=%fused_computation.21 | convolution fusion | flops 4832428032 | bytes 14286848 | tf_op jit(solution)/shard_map/dot_general | solution.py:319
  102.7 10.8 %multiply_convert_fusion = bf16[576,4096]{1,0:T(8,128)(2,1)S(1)} fusion(f32[576,4096]{1,0:T(8,128)} %get-tuple-element.25, bf16[576,1024]{1,0:T(8,128)(2,1)} %bitcast.7, bf16[1,4096,1024]{2,1,0:T(8,128)(2,1)} %param.16), kind=kOutput, calls=%fused_computation | convolution fusion | flops 4853071872 | bytes 23724032 | tf_op jit(solution)/shard_map/dot_general | solution.py:255
  113.6 6.1 %fusion.10 = bf16[576,1024]{1,0:T(8,128)(2,1)} fusion(bf16[576,4096]{1,0:T(8,128)(2,1)S(1)} %multiply_convert_fusion, bf16[1,1024,4096]{2,1,0:T(8,128)(2,1)S(1)} %bitcast.92), kind=kOutput, calls=%fused_computation.20 | convolution fusion | flops 4832428032 | bytes 14286848 | tf_op jit(solution)/shard_map/dot_general | solution.py:255
  119.7 3.4 convolution_convert_fusion.2
  123.1 3.3 convolution_convert_fusion.6
  126.4 3.3 convolution_convert_fusion.7
  129.7 3.5 convolution_convert_fusion.4
  133.1 3.7 %fusion.46 = f32[1024,512]{1,0:T(8,128)} fusion(bf16[576,1024]{1,0:T(8,128)(2,1)} %bitcast.9, bf16[576,4096]{1,0:T(8,128)(2,1)S(1)} %multiply_convert_fusion, s32[]{:T(128)S(6)} %select_n.53), kind=kOutput, calls=%fused_computation.56 | convolution fusion | flops 603979776 | bytes 3866628 | tf_op jit(solution)/shard_map/dot_general | solution.py:251
  136.8 3.8 %fusion.30 = f32[512,1024]{1,0:T(8,128)} fusion(bf16[576,1024]{1,0:T(8,128)(2,1)} %bitcast.7, bf16[576,4096]{1,0:T(8,128)(2,1)} %copy-done.16, s32[]{:T(128)S(6)} %select_n.53), kind=kOutput, calls=%fused_computation.44 | convolution fusion | flops 603979776 | bytes 3866628 | tf_op jit(solution)/shard_map/dot_general | solution.py:251
  140.6 4.5 %all-to-all-start.3 = ((bf16[4,144,1024]{2,1,0:T(8,128)(2,1)}), bf16[4,144,1024]{2,1,0:T(8,128)(2,1)}, u32[]{:S(2)}, u32[]{:S(2)}) async-start(bf16[4,144,1024]{2,1,0:T(8,128)(2,1)} %bitcast.85), calls=%async_computation.3 | async-start | bytes 2359296 | tf_op jit(solution)/shard_map/all_to_all | solution.py:259
  145.2 3.9 %fusion.38 = f32[1024,512]{1,0:T(8,128)} fusion(bf16[576,1024]{1,0:T(8,128)(2,1)} %bitcast.9, bf16[576,4096]{1,0:T(8,128)(2,1)} %copy-done.14, s32[]{:T(128)S(6)} %select_n.57), kind=kOutput, calls=%fused_computation.50 | convolution fusion | flops 603979776 | bytes 3866628 | tf_op jit(solution)/shard_map/dot_general | solution.py:251
  149.5 2.5 convolution_convert_fusion.8
  152.7 3.8 %fusion.22 = f32[512,1024]{1,0:T(8,128)} fusion(bf16[576,1024]{1,0:T(8,128)(2,1)} %bitcast.7, bf16[576,4096]{1,0:T(8,128)(2,1)} %copy-done.16, s32[]{:T(128)S(6)} %select_n.55), kind=kOutput, calls=%fused_computation.38 | convolution fusion | flops 603979776 | bytes 3866628 | tf_op jit(solution)/shard_map/dot_general | solution.py:251
  156.5 3.3 convolution_convert_fusion.9
  159.8 3.3 convolution_convert_fusion.5
  163.1 3.4 convolution_convert_fusion.3
  166.8 3.3 add_convert_fusion.4
  170.0 1.5 collective-permute-start.5
  171.5 3.3 add_convert_fusion.1
  174.8 1.5 collective-permute-start.12
  176.3 3.3 add_convert_fusion.5
  179.6 3.3 add_convert_fusion.2
  182.9 4.8 %all-to-all-start.2 = ((bf16[4,144,1024]{2,1,0:T(8,128)(2,1)}), bf16[4,144,1024]{2,1,0:T(8,128)(2,1)}, u32[]{:S(2)}, u32[]{:S(2)}) async-start(bf16[4,144,1024]{2,1,0:T(8,128)(2,1)} %bitcast.83), calls=%async_computation.2 | async-start | bytes 2359296 | tf_op jit(solution)/shard_map/all_to_all | solution.py:259
  187.6 2.4 convolution_convert_fusion.10.back_ref
  190.4 5.2 %collective-permute-done.5 = bf16[1024,512]{1,0:T(8,128)(2,1)} collective-permute-done((bf16[1024,512]{1,0:T(8,128)(2,1)}, bf16[1024,512]{1,0:T(8,128)(2,1)}, u32[]{:S(2)}, u32[]{:S(2)}) %collective-permute-start.5) | collective-permute-done | bytes 1048608 | tf_op jit(solution)/shard_map/ppermute | solution.py:277
  195.6 1.5 collective-permute-start.2
  197.1 2.9 add_convert_fusion.3
  200.1 1.6 collective-permute-start.9
  202.2 3.1 add_convert_fusion
  205.9 28.2 %conv_backward.1 = (bf16[512,1024]{1,0:T(8,128)(2,1)}, f32[33,1024]{1,0:T(8,128)S(1)}) custom-call(s32[2]{0:T(128)S(1)} %copy-done, bf16[512,1024]{1,0:T(8,128)(2,1)S(1)} %copy-done.1, f32[31,1024]{1,0:T(8,128)S(1)} %copy-done.3, f32[1,1024]{1,0:T(1,128)S(1)} %bitcast.80, f32[1,1024]{1,0:T(1,128)S(1)} %bitcast.82, ...), custom_call_target="tpu_custom_call" | custom-call | flops 8589934592 | bytes 83886080 | tf_op jit(solution)/shard_map/conv_backward/pallas_call | solution.py:223
  234.7 46.8 %psum.15 = f32[2,1024]{1,0:T(2,128)} all-reduce(f32[2,1024]{1,0:T(2,128)S(1)} %slice.15), channel_id=1, replica_groups=mesh['dp'=8,'expert'=4] {'dp','expert'}, use_global_device_ids=true, to_apply=%region_4.5 | all-reduce | flops 2048 | bytes 16384 | tf_op jit(solution)/shard_map/psum | solution.py:327
  281.6 3.4 add_convert_fusion.6
  285.0 4.0 %add_bitcast_fusion.1 = f32[1,1024,512]{2,1,0:T(8,128)} fusion(bf16[1024,512]{1,0:T(8,128)(2,1)} %collective-permute-done.6, bf16[1024,512]{1,0:T(8,128)(2,1)} %collective-permute-done.2, f32[1024,512]{1,0:T(8,128)S(1)} %copy-done.9, bf16[1024,512]{1,0:T(8,128)(2,1)} %collective-permute-done), kind=kLoop, calls=%fused_computation.15 | loop fusion | flops 3145728 | bytes 7340032 | tf_op jit(solution)/shard_map/broadcast_in_dim | solution.py:328
  289.0 3.9 %add_bitcast_fusion = f32[1,512,1024]{2,1,0:T(8,128)} fusion(bf16[512,1024]{1,0:T(8,128)(2,1)} %collective-permute-done.13, bf16[512,1024]{1,0:T(8,128)(2,1)} %collective-permute-done.9, f32[512,1024]{1,0:T(8,128)S(1)} %copy-done.8, bf16[512,1024]{1,0:T(8,128)(2,1)} %collective-permute-done.7), kind=kLoop, calls=%fused_computation.11 | loop fusion | flops 3145728 | bytes 7340032 | tf_op jit(solution)/shard_map/broadcast_in_dim | solution.py:328
  292.9 65.7 %all-reduce.2.cloned.1.call-done = f32[31,1024]{1,0:T(8,128)} async-done(((f32[31,1024]{1,0:T(8,128)}), f32[31,1024]{1,0:T(8,128)}) %all-reduce.2.cloned.1.call-update) | async-done | bytes 126992 | tf_op jit(solution)/shard_map/psum | solution.py:327
  358.6 1.6 copy.19
  (80 shorter events, 4.9 us)
Async XLA Ops:
  11.0 9.5 %copy-start = (s32[2]{0:T(128)S(1)}, s32[2]{0:T(128)}, u32[]{:S(2)}) copy-start(s32[2]{0:T(128)} %len_ref.3) | copy-start | bytes 28
  11.0 9.5 %copy-start.1 = (bf16[512,1024]{1,0:T(8,128)(2,1)S(1)}, bf16[512,1024]{1,0:T(8,128)(2,1)}, u32[]{:S(2)}) copy-start(bf16[512,1024]{1,0:T(8,128)(2,1)} %x_ref.3) | copy-start | bytes 3145732
  11.0 9.5 %copy-start.3 = (f32[31,1024]{1,0:T(8,128)S(1)}, f32[31,1024]{1,0:T(8,128)}, u32[]{:S(2)}) copy-start(f32[31,1024]{1,0:T(8,128)} %taps_ref.3) | copy-start | bytes 380932
  11.1 9.5 %copy-start.4 = (f32[1024]{0:T(1024)S(1)}, f32[1024]{0:T(1024)}, u32[]{:S(2)}) copy-start(f32[1024]{0:T(1024)} %param.13) | copy-start | bytes 12292
  11.1 9.5 %copy-start.5 = (f32[1024]{0:T(1024)S(1)}, f32[1024]{0:T(1024)}, u32[]{:S(2)}) copy-start(f32[1024]{0:T(1024)} %param.14) | copy-start | bytes 12292
  14.2 35.0 %all-to-all-start = ((bf16[4,144,1024]{2,1,0:T(8,128)(2,1)}), bf16[4,144,1024]{2,1,0:T(8,128)(2,1)}, u32[]{:S(2)}, u32[]{:S(2)}) async-start(bf16[4,144,1024]{2,1,0:T(8,128)(2,1)} %bitcast.6), calls=%async_computation | async-start | bytes 2359296 | tf_op jit(solution)/shard_map/all_to_all | solution.py:259
  34.8 1.3 copy-start.6
  49.2 32.4 %all-to-all-start.1 = ((bf16[4,144,1024]{2,1,0:T(8,128)(2,1)}), bf16[4,144,1024]{2,1,0:T(8,128)(2,1)}, u32[]{:S(2)}, u32[]{:S(2)}) async-start(bf16[4,144,1024]{2,1,0:T(8,128)(2,1)} %bitcast.84), calls=%async_computation.1 | async-start | bytes 2359296 | tf_op jit(solution)/shard_map/all_to_all | solution.py:259
  92.3 10.4 %copy-start.16 = (bf16[576,4096]{1,0:T(8,128)(2,1)}, bf16[576,4096]{1,0:T(8,128)(2,1)S(1)}, u32[]{:S(2)}) copy-start(bf16[576,4096]{1,0:T(8,128)(2,1)S(1)} %get-tuple-element.24) | copy-start | bytes 14155780
  92.3 21.2 %slice-start = ((s8[8388608]{0:T(1024)(128)(4,1)}), s8[4194304]{0:T(1024)(128)(4,1)S(1)}, s32[]{:S(2)}) async-start(s8[8388608]{0:T(1024)(128)(4,1)} %bitcast.91), calls=%async_computation.5 | async-start | bytes 8388608
  102.7 10.8 %slice-start.1 = ((s8[8388608]{0:T(1024)(128)(4,1)}), s8[4194304]{0:T(1024)(128)(4,1)S(1)}, s32[]{:S(2)}) async-start(s8[8388608]{0:T(1024)(128)(4,1)} %bitcast.91), calls=%async_computation.6 | async-start | bytes 8388608
  113.6 19.5 %copy-start.14 = (bf16[576,4096]{1,0:T(8,128)(2,1)}, bf16[576,4096]{1,0:T(8,128)(2,1)S(1)}, u32[]{:S(2)}) copy-start(bf16[576,4096]{1,0:T(8,128)(2,1)S(1)} %multiply_convert_fusion) | copy-start | bytes 14155780
  140.6 42.3 %all-to-all-start.3 = ((bf16[4,144,1024]{2,1,0:T(8,128)(2,1)}), bf16[4,144,1024]{2,1,0:T(8,128)(2,1)}, u32[]{:S(2)}, u32[]{:S(2)}) async-start(bf16[4,144,1024]{2,1,0:T(8,128)(2,1)} %bitcast.85), calls=%async_computation.3 | async-start | bytes 2359296 | tf_op jit(solution)/shard_map/all_to_all | solution.py:259
  145.1 4.3 %copy-start.15 = (bf16[576,4096]{1,0:T(8,128)(2,1)S(1)}, bf16[576,4096]{1,0:T(8,128)(2,1)}, u32[]{:S(2)}) copy-start(bf16[576,4096]{1,0:T(8,128)(2,1)} %copy-done.14) | copy-start | bytes 14155780
  145.1 21.3 %collective-permute-start.4 = (bf16[1024,512]{1,0:T(8,128)(2,1)}, bf16[1024,512]{1,0:T(8,128)(2,1)S(1)}, u32[]{:S(2)}, u32[]{:S(2)}) collective-permute-start(bf16[1024,512]{1,0:T(8,128)(2,1)} %convolution_convert_fusion.6), channel_id=1, source_target_pairs={{0,4},{4,0},{8,12},{12,8},{16,20},{20,16},{24,28},{28,24},{1,5},{5... | collective-permute-start | bytes 3145736 | tf_op jit(solution)/shard_map/ppermute | solution.py:277
  149.1 3.1 copy-start.13
  149.1 3.4 copy-start.12
  149.1 41.0 %collective-permute-start.3 = (bf16[1024,512]{1,0:T(8,128)(2,1)}, bf16[1024,512]{1,0:T(8,128)(2,1)}, u32[]{:S(2)}, u32[]{:S(2)}) collective-permute-start(bf16[1024,512]{1,0:T(8,128)(2,1)} %convolution_convert_fusion.7), channel_id=1, source_target_pairs={{0,4},{4,0},{8,12},{12,8},{16,20},{20,16},{24,28},{28,24},{1,5},{5... | collective-permute-start | bytes 3145736 | tf_op jit(solution)/shard_map/ppermute | solution.py:277
  149.5 10.3 %slice-start.2 = ((s8[4718592]{0:T(1024)(128)(4,1)}), s8[4194304]{0:T(1024)(128)(4,1)S(1)}, s32[]{:S(2)}) async-start(s8[4718592]{0:T(1024)(128)(4,1)} %bitcast.93), calls=%async_computation.7 | async-start | bytes 8388608
  152.0 7.9 %slice-start.3 = ((s8[4718592]{0:T(1024)(128)(4,1)}), s8[524288]{0:T(1024)(128)(4,1)S(1)}, s32[]{:S(2)}) async-start(s8[4718592]{0:T(1024)(128)(4,1)} %bitcast.93), calls=%async_computation.8 | async-start | bytes 1048576
  152.0 22.8 %collective-permute-start.1 = (bf16[1024,512]{1,0:T(8,128)(2,1)S(1)}, bf16[1024,512]{1,0:T(8,128)(2,1)S(1)}, u32[]{:S(2)}, u32[]{:S(2)}) collective-permute-start(bf16[1024,512]{1,0:T(8,128)(2,1)S(1)} %convolution_convert_fusion.8), channel_id=1, source_target_pairs={{0,4},{4,0},{8,12},{12,8},{16,20},{20,16},{24,28},{28,24},{1,5},{5... | collective-permute-start | bytes 3145736 | tf_op jit(solution)/shard_map/ppermute | solution.py:277
  152.2 17.8 %collective-permute-start.11 = (bf16[512,1024]{1,0:T(8,128)(2,1)S(1)}, bf16[512,1024]{1,0:T(8,128)(2,1)S(1)}, u32[]{:S(2)}, u32[]{:S(2)}) collective-permute-start(bf16[512,1024]{1,0:T(8,128)(2,1)S(1)} %copy-done.13), channel_id=1, source_target_pairs={{0,4},{4,0},{8,12},{12,8},{16,20},{20,16},{24,28},{28,24},{1,5},{5... | collective-permute-start | bytes 3145736 | tf_op jit(solution)/shard_map/ppermute | solution.py:277
  152.5 27.0 %collective-permute-start.8 = (bf16[512,1024]{1,0:T(8,128)(2,1)S(1)}, bf16[512,1024]{1,0:T(8,128)(2,1)S(1)}, u32[]{:S(2)}, u32[]{:S(2)}) collective-permute-start(bf16[512,1024]{1,0:T(8,128)(2,1)S(1)} %copy-done.12), channel_id=1, source_target_pairs={{0,4},{4,0},{8,12},{12,8},{16,20},{20,16},{24,28},{28,24},{1,5},{5... | collective-permute-start | bytes 3145736 | tf_op jit(solution)/shard_map/ppermute | solution.py:277
  166.5 33.6 %collective-permute-start.10 = (bf16[512,1024]{1,0:T(8,128)(2,1)}, bf16[512,1024]{1,0:T(8,128)(2,1)}, u32[]{:S(2)}, u32[]{:S(2)}) collective-permute-start(bf16[512,1024]{1,0:T(8,128)(2,1)} %convolution_convert_fusion.3), channel_id=1, source_target_pairs={{0,4},{4,0},{8,12},{12,8},{16,20},{20,16},{24,28},{28,24},{1,5},{5... | collective-permute-start | bytes 3145736 | tf_op jit(solution)/shard_map/ppermute | solution.py:277
  170.0 25.6 %collective-permute-start.5 = (bf16[1024,512]{1,0:T(8,128)(2,1)}, bf16[1024,512]{1,0:T(8,128)(2,1)}, u32[]{:S(2)}, u32[]{:S(2)}) collective-permute-start(bf16[1024,512]{1,0:T(8,128)(2,1)} %add_convert_fusion.4), channel_id=1, source_target_pairs={{0,8},{4,12},{8,0},{12,4},{16,24},{20,28},{24,16},{28,20},{1,9},{5... | collective-permute-start | bytes 3145736 | tf_op jit(solution)/shard_map/ppermute | solution.py:277
  174.8 26.9 %collective-permute-start.12 = (bf16[512,1024]{1,0:T(8,128)(2,1)}, bf16[512,1024]{1,0:T(8,128)(2,1)}, u32[]{:S(2)}, u32[]{:S(2)}) collective-permute-start(bf16[512,1024]{1,0:T(8,128)(2,1)} %add_convert_fusion.1), channel_id=1, source_target_pairs={{0,16},{4,20},{8,24},{12,28},{16,0},{20,4},{24,8},{28,12},{1,17},{... | collective-permute-start | bytes 3145736 | tf_op jit(solution)/shard_map/ppermute | solution.py:277
  179.6 25.7 %collective-permute-start = (bf16[1024,512]{1,0:T(8,128)(2,1)}, bf16[1024,512]{1,0:T(8,128)(2,1)}, u32[]{:S(2)}, u32[]{:S(2)}) collective-permute-start(bf16[1024,512]{1,0:T(8,128)(2,1)} %convolution_convert_fusion.9), channel_id=1, source_target_pairs={{0,4},{4,0},{8,12},{12,8},{16,20},{20,16},{24,28},{28,24},{1,5},{5... | collective-permute-start | bytes 3145736 | tf_op jit(solution)/shard_map/ppermute | solution.py:277
  182.9 98.7 %all-to-all-start.2 = ((bf16[4,144,1024]{2,1,0:T(8,128)(2,1)}), bf16[4,144,1024]{2,1,0:T(8,128)(2,1)}, u32[]{:S(2)}, u32[]{:S(2)}) async-start(bf16[4,144,1024]{2,1,0:T(8,128)(2,1)} %bitcast.83), calls=%async_computation.2 | async-start | bytes 2359296 | tf_op jit(solution)/shard_map/all_to_all | solution.py:259
  187.6 170.9 %all-reduce.2.cloned.1.call-start = ((), (), s32[]{:S(2)}) async-start(), calls=%async_computation.4 | async-start | bytes 262144 | tf_op jit(solution)/shard_map/psum | solution.py:327
  187.6 9.5 %copy-start.11 = (f32[1024,512]{1,0:T(8,128)S(1)}, f32[1024,512]{1,0:T(8,128)}, u32[]{:S(2)}) copy-start(f32[1024,512]{1,0:T(8,128)} %fusion.38) | copy-start | bytes 6291460
  190.1 12.1 %copy-start.10 = (f32[512,1024]{1,0:T(8,128)S(1)}, f32[512,1024]{1,0:T(8,128)}, u32[]{:S(2)}) copy-start(f32[512,1024]{1,0:T(8,128)} %fusion.22) | copy-start | bytes 6291460
  190.1 98.9 %collective-permute-start.7 = (bf16[512,1024]{1,0:T(8,128)(2,1)}, bf16[512,1024]{1,0:T(8,128)(2,1)}, u32[]{:S(2)}, u32[]{:S(2)}) collective-permute-start(bf16[512,1024]{1,0:T(8,128)(2,1)} %convolution_convert_fusion.5), channel_id=1, source_target_pairs={{0,4},{4,0},{8,12},{12,8},{16,20},{20,16},{24,28},{28,24},{1,5},{5... | collective-permute-start | bytes 3145736 | tf_op jit(solution)/shard_map/ppermute | solution.py:277
  195.6 89.4 %collective-permute-start.2 = (bf16[1024,512]{1,0:T(8,128)(2,1)}, bf16[1024,512]{1,0:T(8,128)(2,1)}, u32[]{:S(2)}, u32[]{:S(2)}) collective-permute-start(bf16[1024,512]{1,0:T(8,128)(2,1)} %add_convert_fusion.5), channel_id=1, source_target_pairs={{0,8},{4,12},{8,0},{12,4},{16,24},{20,28},{24,16},{28,20},{1,9},{5... | collective-permute-start | bytes 3145736 | tf_op jit(solution)/shard_map/ppermute | solution.py:277
  200.1 5.8 %copy-start.2 = (bf16[512,1024]{1,0:T(8,128)(2,1)S(1)}, bf16[512,1024]{1,0:T(8,128)(2,1)}, u32[]{:S(2)}) copy-start(bf16[512,1024]{1,0:T(8,128)(2,1)} %grad_ref.1) | copy-start | bytes 3145732
  200.1 5.8 %copy-start.7 = (f32[512,1024]{1,0:T(8,128)S(1)}, f32[512,1024]{1,0:T(8,128)}, u32[]{:S(2)}) copy-start(f32[512,1024]{1,0:T(8,128)} %copy-done.6) | copy-start | bytes 6291460
  200.1 88.9 %collective-permute-start.9 = (bf16[512,1024]{1,0:T(8,128)(2,1)}, bf16[512,1024]{1,0:T(8,128)(2,1)}, u32[]{:S(2)}, u32[]{:S(2)}) collective-permute-start(bf16[512,1024]{1,0:T(8,128)(2,1)} %add_convert_fusion.2), channel_id=1, source_target_pairs={{0,16},{4,20},{8,24},{12,28},{16,0},{20,4},{24,8},{28,12},{1,17},{... | collective-permute-start | bytes 3145736 | tf_op jit(solution)/shard_map/ppermute | solution.py:277
  201.7 83.3 %collective-permute-start.6 = (bf16[1024,512]{1,0:T(8,128)(2,1)}, bf16[1024,512]{1,0:T(8,128)(2,1)}, u32[]{:S(2)}, u32[]{:S(2)}) collective-permute-start(bf16[1024,512]{1,0:T(8,128)(2,1)} %add_convert_fusion.3), channel_id=1, source_target_pairs={{0,16},{4,20},{8,24},{12,28},{16,0},{20,4},{24,8},{28,12},{1,17},{... | collective-permute-start | bytes 3145736 | tf_op jit(solution)/shard_map/ppermute | solution.py:277
  205.3 83.7 %collective-permute-start.13 = (bf16[512,1024]{1,0:T(8,128)(2,1)}, bf16[512,1024]{1,0:T(8,128)(2,1)}, u32[]{:S(2)}, u32[]{:S(2)}) collective-permute-start(bf16[512,1024]{1,0:T(8,128)(2,1)} %add_convert_fusion), channel_id=1, source_target_pairs={{0,8},{4,12},{8,0},{12,4},{16,24},{20,28},{24,16},{28,20},{1,9},{5... | collective-permute-start | bytes 3145736 | tf_op jit(solution)/shard_map/ppermute | solution.py:277
  281.6 3.4 copy-start.9
  285.0 4.0 %copy-start.8 = (f32[512,1024]{1,0:T(8,128)S(1)}, f32[512,1024]{1,0:T(8,128)}, u32[]{:S(2)}) copy-start(f32[512,1024]{1,0:T(8,128)} %fusion.30) | copy-start | bytes 6291460
Sparse Core Ops, SparseCore 0:
  234.8 123.6 all-reduce.1
